TPU v7x, 512 devices: a whole 4x4x16 slice. The times are simulated.
512 devices in a mesh: tm: 32 (over x_lo, z), space: 16 (over x_hi, y, core).
Axes of the slice: x: 4 (x_hi: 2, x_lo: 2; x = x_hi * 2 + x_lo), y: 4, z: 16, core: 2. Of those that a mesh axis runs over, the one named last changes fastest.
Arguments:
- iterate: float32 [32, 512, 4096], P('tm', 'space'), may hold values from -6 to 6
- source: float32 [32, 512, 4096], P('tm', 'space'), may hold values from -6 to 6
- conduct: float32 [512, 4096], P('space'), may hold values from 0.2 to 5
Outputs:
- updated: float32 [32, 512, 4096], P('tm', 'space')
All inputs are finite; a program needn't handle non-finite values.
Results may differ from a plain program's by a relative error of at most 0.0003.
Values sent between devices are 32-bit elements; how exact they have to be, the bound alone decides.
A program may use at most 64 MiB of HBM per device.

v0:
```python
import jax
import jax.numpy as jnp
from jax import lax
from jax.sharding import PartitionSpec as P

SWEEPS = 8


ALPHA = 0.05
OMEGA = 0.8


def with_halo(x, sides, width):
    for axis, dim in sides:
        count, length = (lax.axis_size(axis), x.shape[dim])
        up = [(i, (i + 1) % count) for i in range(count - 1)]
        down = [(j, i) for i, j in up]
        last = lax.slice_in_dim(x, length - width, length, axis=dim)
        leading = lax.slice_in_dim(x, 0, width, axis=dim)
        before = lax.ppermute(last, axis, up)
        after = lax.ppermute(leading, axis, down)
        x = jnp.concatenate([before, x, after], axis=dim)
    return x


def from_behind(value, axis, steps):
    count = lax.axis_size(axis)
    leading, last = (max(0, -steps), min(count, count - steps))
    return lax.ppermute(value, axis, [(source, source + steps) for source in range(leading, last)])


def face_terms(conduct_rows):
    middle = conduct_rows[1:-1]
    up_face = 0.5 * (middle + conduct_rows[:-2])
    down_face = 0.5 * (middle + conduct_rows[2:])
    padded = jnp.pad(middle, ((0, 0), (1, 1)))
    left_face = 0.5 * (middle + padded[:, :-2])
    right_face = 0.5 * (middle + padded[:, 2:])
    return (up_face, down_face, left_face, right_face)


def neighbours(extended, face_set):
    up_face, down_face, left_face, right_face = face_set
    middle = extended[..., 1:-1, :]
    widths = [(0, 0)] * (middle.ndim - 1) + [(1, 1)]
    padded = jnp.pad(middle, widths)
    return (
        up_face * extended[..., :-2, :]
        + down_face * extended[..., 2:, :]
        + left_face * padded[..., :-2]
        + right_face * padded[..., 2:]
    )


def relax_sweep(extended, spectrum, face_set, inverse_real, inverse_imag):
    combined = spectrum + neighbours(extended, face_set)
    update_real = inverse_real * combined[0] - inverse_imag * combined[1]
    update_imag = inverse_real * combined[1] + inverse_imag * combined[0]
    return (1.0 - OMEGA) * extended[:, 1:-1] + OMEGA * jnp.stack([update_real, update_imag])


def shifted_inverse(frequency, total_steps, diagonal_sum):
    root_alpha = jnp.power(jnp.float32(ALPHA), jnp.float32(1.0) / total_steps)
    phase_angle = 2.0 * jnp.pi * frequency.astype(jnp.float32) / total_steps
    shift_real = 1.0 - root_alpha * jnp.cos(phase_angle)
    shift_imag = root_alpha * jnp.sin(phase_angle)
    shifted = shift_real + diagonal_sum
    magnitude = shifted * shifted + shift_imag * shift_imag
    return (shifted / magnitude, -shift_imag / magnitude)


def dft_tables(total_steps):
    index_row = jnp.arange(total_steps, dtype=jnp.int32)
    product = index_row[:, None] * index_row[None, :] % total_steps
    phase_table = 2.0 * jnp.pi * product.astype(jnp.float32) / total_steps
    return (jnp.cos(phase_table), jnp.sin(phase_table))


def per_device(iterate, source, conduct):
    tm_size = lax.axis_size("tm")
    tm_rank = lax.axis_index("tm")
    row_count = conduct.shape[0]
    highest = lax.Precision.HIGHEST
    rim_width = 1
    stacked = jnp.stack([conduct, iterate[0]])
    extended = with_halo(stacked, (("space", 1),), rim_width)
    face_all = face_terms(extended[0])
    diagonal_all = face_all[0] + face_all[1] + face_all[2] + face_all[3]
    lead = rim_width - 1
    face_set = tuple((face_part for face_part in face_all))
    own_rim = extended[1, lead : lead + row_count + 2]
    applied = neighbours(own_rim, face_set) - diagonal_all * iterate[0]
    previous = from_behind(iterate, "tm", 1)
    residual = source[0] - iterate[0] + previous[0] + applied
    weighting = jnp.power(jnp.float32(ALPHA), tm_rank.astype(jnp.float32) / tm_size)
    scaled = residual * weighting
    cosine_table, sine_table = dft_tables(tm_size)
    columns = lax.all_to_all(scaled[None], "tm", split_axis=1, concat_axis=0, tiled=True)
    spec_real = jnp.einsum("jn,nrc->jrc", cosine_table, columns, precision=highest)
    spec_imag = -jnp.einsum("jn,nrc->jrc", sine_table, columns, precision=highest)
    spectrum = lax.all_to_all(
        jnp.stack([spec_real, spec_imag]), "tm", split_axis=1, concat_axis=2, tiled=True
    )[:, 0]
    inverse_real, inverse_imag = shifted_inverse(tm_rank, tm_size, diagonal_all)
    solved = jnp.zeros_like(spectrum)
    for sweep_idx in range(SWEEPS):
        solved_rim = with_halo(solved, (("space", 1),), 1)
        solved = relax_sweep(solved_rim, spectrum, face_set, inverse_real, inverse_imag)
    cosine_table, sine_table = dft_tables(tm_size)
    spread = lax.all_to_all(solved[:, None], "tm", split_axis=2, concat_axis=1, tiled=True)
    inverse = jnp.einsum("nj,jrc->nrc", cosine_table, spread[0], precision=highest) - jnp.einsum(
        "nj,jrc->nrc", sine_table, spread[1], precision=highest
    )
    real_part = lax.all_to_all(inverse, "tm", split_axis=0, concat_axis=1, tiled=True)[0]
    correction = real_part / tm_size / weighting
    return iterate + correction[None]


def solution(mesh):
    return jax.shard_map(
        per_device,
        mesh=mesh,
        in_specs=(P("tm", "space", None), P("tm", "space", None), P("space", None)),
        out_specs=P("tm", "space", None),
        check_vma=False,
    )
```

profile of v0, /device:TPU:57, one launch (start us, length us, event | category | flops | bytes accessed | tf_op | source)
XLA Modules:
  0.0 320.6 jit_solution(3840180619511623834)
XLA Ops:
  0.0 3.7 %collective-permute-start.2 = (f32[1,32,4096]{2,1,0:T(8,128)}, f32[1,32,4096]{2,1,0:T(8,128)S(1)}, u32[]{:S(2)}, u32[]{:S(2)}) collective-permute-start(f32[1,32,4096]{2,1,0:T(8,128)} %param.3), channel_id=1, source_target_pairs={{0,16},{16,32},{32,48},{48,64},{64,80},{80,96},{96,112},{112,128},... | collective-permute-start | bytes 1572872 | tf_op jit(solution)/shard_map/ppermute | solution.py:29
  4.8 5.2 %collective-permute-start = (f32[2,1,4096]{2,1,0:T(1,128)S(1)}, f32[2,1,4096]{2,1,0:T(1,128)S(1)}, u32[]{:S(2)}, u32[]{:S(2)}) collective-permute-start(f32[2,1,4096]{2,1,0:T(1,128)S(1)} %get-tuple-element.39), channel_id=1, source_target_pairs={{0,1},{1,2},{2,3},{3,4},{4,5},{5,6},{6,7},{7,8},{8,9},{9,10},{10,1... | collective-permute-start | bytes 98312 | tf_op jit(solution)/shard_map/ppermute | solution.py:20
  12.0 6.9 %collective-permute-done.1 = f32[2,1,4096]{2,1,0:T(1,128)S(1)} collective-permute-done((f32[2,1,4096]{2,1,0:T(1,128)S(1)}, f32[2,1,4096]{2,1,0:T(1,128)S(1)}, u32[]{:S(2)}, u32[]{:S(2)}) %collective-permute-start.1) | collective-permute-done | bytes 32800 | tf_op jit(solution)/shard_map/ppermute | solution.py:21
  21.2 44.5 %all_to_all.16 = f32[1,32,4096]{2,0,1:T(1,128)S(1)} all-to-all(f32[1,32,4096]{2,0,1:T(1,128)S(1)} %broadcast_in_dim.4), channel_id=1, replica_groups=mesh['tm'=32,'space'=16] {'tm'}, dimensions={1} | all-to-all | bytes 1048576 | tf_op jit(solution)/shard_map/all_to_all | solution.py:98
  69.6 5.7 %all-to-all-start.1 = ((f32[2,32,1,4096]{3,2,0,1:T(1,128)}), f32[2,32,1,4096]{3,2,0,1:T(1,128)S(1)}, u32[]{:S(2)}, u32[]{:S(2)}) async-start(f32[2,32,1,4096]{3,2,0,1:T(1,128)} %copy.4), calls=%async_computation.1 | async-start | bytes 2097152 | tf_op jit(solution)/shard_map/all_to_all | solution.py:101
  75.4 3.0 collective-permute-start.4
  78.4 6.1 %collective-permute-start.3 = (f32[2,1,4096]{2,1,0:T(1,128)S(1)}, f32[2,1,4096]{2,1,0:T(1,128)S(1)}, u32[]{:S(2)}, u32[]{:S(2)}) collective-permute-start(f32[2,1,4096]{2,1,0:T(1,128)S(1)} %broadcast.181), channel_id=1, source_target_pairs={{0,1},{1,2},{2,3},{3,4},{4,5},{5,6},{6,7},{7,8},{8,9},{9,10},{10,1... | collective-permute-start | bytes 98312 | tf_op jit(solution)/shard_map/ppermute | solution.py:20
  86.9 43.3 %all-to-all-done.1 = f32[2,32,1,4096]{3,2,0,1:T(1,128)S(1)} async-done(((f32[2,32,1,4096]{3,2,0,1:T(1,128)}), f32[2,32,1,4096]{3,2,0,1:T(1,128)S(1)}, u32[]{:S(2)}, u32[]{:S(2)}) %all-to-all-start.1) | async-done | bytes 1048608 | tf_op jit(solution)/shard_map/all_to_all | solution.py:101
  132.2 3.9 %collective-permute-start.5 = (f32[2,1,4096]{2,1,0:T(1,128)S(1)}, f32[2,1,4096]{2,1,0:T(1,128)S(1)}, u32[]{:S(2)}, u32[]{:S(2)}) collective-permute-start(f32[2,1,4096]{2,1,0:T(1,128)S(1)} %get-tuple-element.35), channel_id=1, source_target_pairs={{0,1},{1,2},{2,3},{3,4},{4,5},{5,6},{6,7},{7,8},{8,9},{9,10},{10,1... | collective-permute-start | bytes 98312 | tf_op jit(solution)/shard_map/ppermute | solution.py:20
  138.1 6.9 %collective-permute-done.6 = f32[2,1,4096]{2,1,0:T(1,128)S(1)} collective-permute-done((f32[2,1,4096]{2,1,0:T(1,128)S(1)}, f32[2,1,4096]{2,1,0:T(1,128)S(1)}, u32[]{:S(2)}, u32[]{:S(2)}) %collective-permute-start.6) | collective-permute-done | bytes 32800 | tf_op jit(solution)/shard_map/ppermute | solution.py:21
  148.6 2.4 collective-permute-start.8
  151.1 6.4 %collective-permute-done.8 = f32[2,1,4096]{2,1,0:T(1,128)S(1)} collective-permute-done((f32[2,1,4096]{2,1,0:T(1,128)S(1)}, f32[2,1,4096]{2,1,0:T(1,128)S(1)}, u32[]{:S(2)}, u32[]{:S(2)}) %collective-permute-start.8) | collective-permute-done | bytes 32800 | tf_op jit(solution)/shard_map/ppermute | solution.py:21
  161.3 2.6 collective-permute-start.10
  163.9 6.2 %collective-permute-done.10 = f32[2,1,4096]{2,1,0:T(1,128)S(1)} collective-permute-done((f32[2,1,4096]{2,1,0:T(1,128)S(1)}, f32[2,1,4096]{2,1,0:T(1,128)S(1)}, u32[]{:S(2)}, u32[]{:S(2)}) %collective-permute-start.10) | collective-permute-done | bytes 32800 | tf_op jit(solution)/shard_map/ppermute | solution.py:21
  174.0 2.4 collective-permute-start.12
  176.4 6.4 %collective-permute-done.12 = f32[2,1,4096]{2,1,0:T(1,128)S(1)} collective-permute-done((f32[2,1,4096]{2,1,0:T(1,128)S(1)}, f32[2,1,4096]{2,1,0:T(1,128)S(1)}, u32[]{:S(2)}, u32[]{:S(2)}) %collective-permute-start.12) | collective-permute-done | bytes 32800 | tf_op jit(solution)/shard_map/ppermute | solution.py:21
  186.9 2.4 collective-permute-start.14
  189.3 6.4 %collective-permute-done.14 = f32[2,1,4096]{2,1,0:T(1,128)S(1)} collective-permute-done((f32[2,1,4096]{2,1,0:T(1,128)S(1)}, f32[2,1,4096]{2,1,0:T(1,128)S(1)}, u32[]{:S(2)}, u32[]{:S(2)}) %collective-permute-start.14) | collective-permute-done | bytes 32800 | tf_op jit(solution)/shard_map/ppermute | solution.py:21
  199.9 2.4 collective-permute-start.16
  202.3 6.4 %collective-permute-done.16 = f32[2,1,4096]{2,1,0:T(1,128)S(1)} collective-permute-done((f32[2,1,4096]{2,1,0:T(1,128)S(1)}, f32[2,1,4096]{2,1,0:T(1,128)S(1)}, u32[]{:S(2)}, u32[]{:S(2)}) %collective-permute-start.16) | collective-permute-done | bytes 32800 | tf_op jit(solution)/shard_map/ppermute | solution.py:21
  213.0 2.6 collective-permute-start.18
  215.7 6.2 %collective-permute-done.18 = f32[2,1,4096]{2,1,0:T(1,128)S(1)} collective-permute-done((f32[2,1,4096]{2,1,0:T(1,128)S(1)}, f32[2,1,4096]{2,1,0:T(1,128)S(1)}, u32[]{:S(2)}, u32[]{:S(2)}) %collective-permute-start.18) | collective-permute-done | bytes 32800 | tf_op jit(solution)/shard_map/ppermute | solution.py:21
  225.4 54.5 %all_to_all.17 = f32[2,1,32,4096]{3,1,0,2:T(1,128)S(1)} all-to-all(f32[2,1,32,4096]{3,1,0,2:T(1,128)S(1)} %copy.6), channel_id=1, replica_groups=mesh['tm'=32,'space'=16] {'tm'}, dimensions={2} | all-to-all | bytes 2097152 | tf_op jit(solution)/shard_map/all_to_all | solution.py:110
  282.3 36.5 %all_to_all.18 = f32[32,1,4096]{2,1,0:T(1,128)S(1)} all-to-all(f32[32,1,4096]{2,1,0:T(1,128)S(1)} %copy.7), channel_id=1, replica_groups=mesh['tm'=32,'space'=16] {'tm'}, dimensions={0} | all-to-all | bytes 1048576 | tf_op jit(solution)/shard_map/all_to_all | solution.py:114
  (78 shorter events, 46.7 us)
Async XLA Ops:
  0.0 18.8 %copy-start.2 = (f32[1,32,4096]{2,1,0:T(8,128)S(1)}, f32[1,32,4096]{2,1,0:T(8,128)}, u32[]{:S(2)}) copy-start(f32[1,32,4096]{2,1,0:T(8,128)} %param.3) | copy-start | bytes 1572868
  0.0 18.8 %copy-start = (f32[32,4096]{1,0:T(8,128)S(1)}, f32[32,4096]{1,0:T(8,128)}, u32[]{:S(2)}) copy-start(f32[32,4096]{1,0:T(8,128)} %param.5) | copy-start | bytes 1572868
  0.0 18.8 %collective-permute-start.2 = (f32[1,32,4096]{2,1,0:T(8,128)}, f32[1,32,4096]{2,1,0:T(8,128)S(1)}, u32[]{:S(2)}, u32[]{:S(2)}) collective-permute-start(f32[1,32,4096]{2,1,0:T(8,128)} %param.3), channel_id=1, source_target_pairs={{0,16},{16,32},{32,48},{48,64},{64,80},{80,96},{96,112},{112,128},... | collective-permute-start | bytes 1572872 | tf_op jit(solution)/shard_map/ppermute | solution.py:29
  4.8 7.1 %collective-permute-start = (f32[2,1,4096]{2,1,0:T(1,128)S(1)}, f32[2,1,4096]{2,1,0:T(1,128)S(1)}, u32[]{:S(2)}, u32[]{:S(2)}) collective-permute-start(f32[2,1,4096]{2,1,0:T(1,128)S(1)} %get-tuple-element.39), channel_id=1, source_target_pairs={{0,1},{1,2},{2,3},{3,4},{4,5},{5,6},{6,7},{7,8},{8,9},{9,10},{10,1... | collective-permute-start | bytes 98312 | tf_op jit(solution)/shard_map/ppermute | solution.py:20
  10.0 8.8 %collective-permute-start.1 = (f32[2,1,4096]{2,1,0:T(1,128)S(1)}, f32[2,1,4096]{2,1,0:T(1,128)S(1)}, u32[]{:S(2)}, u32[]{:S(2)}) collective-permute-start(f32[2,1,4096]{2,1,0:T(1,128)S(1)} %get-tuple-element.40), channel_id=1, source_target_pairs={{1,0},{2,1},{3,2},{4,3},{5,4},{6,5},{7,6},{8,7},{9,8},{10,9},{11,1... | collective-permute-start | bytes 98312 | tf_op jit(solution)/shard_map/ppermute | solution.py:21
  69.6 60.6 %all-to-all-start.1 = ((f32[2,32,1,4096]{3,2,0,1:T(1,128)}), f32[2,32,1,4096]{3,2,0,1:T(1,128)S(1)}, u32[]{:S(2)}, u32[]{:S(2)}) async-start(f32[2,32,1,4096]{3,2,0,1:T(1,128)} %copy.4), calls=%async_computation.1 | async-start | bytes 2097152 | tf_op jit(solution)/shard_map/all_to_all | solution.py:101
  75.4 11.5 %collective-permute-start.4 = (f32[2,1,4096]{2,1,0:T(1,128)S(1)}, f32[2,1,4096]{2,1,0:T(1,128)S(1)}, u32[]{:S(2)}, u32[]{:S(2)}) collective-permute-start(f32[2,1,4096]{2,1,0:T(1,128)S(1)} %broadcast.181), channel_id=1, source_target_pairs={{1,0},{2,1},{3,2},{4,3},{5,4},{6,5},{7,6},{8,7},{9,8},{10,9},{11,1... | collective-permute-start | bytes 98312 | tf_op jit(solution)/shard_map/ppermute | solution.py:21
  78.4 8.4 %collective-permute-start.3 = (f32[2,1,4096]{2,1,0:T(1,128)S(1)}, f32[2,1,4096]{2,1,0:T(1,128)S(1)}, u32[]{:S(2)}, u32[]{:S(2)}) collective-permute-start(f32[2,1,4096]{2,1,0:T(1,128)S(1)} %broadcast.181), channel_id=1, source_target_pairs={{0,1},{1,2},{2,3},{3,4},{4,5},{5,6},{6,7},{7,8},{8,9},{9,10},{10,1... | collective-permute-start | bytes 98312 | tf_op jit(solution)/shard_map/ppermute | solution.py:20
  130.2 1.0 copy-start.1
  130.2 1.2 copy-start.3
  132.2 5.8 %collective-permute-start.5 = (f32[2,1,4096]{2,1,0:T(1,128)S(1)}, f32[2,1,4096]{2,1,0:T(1,128)S(1)}, u32[]{:S(2)}, u32[]{:S(2)}) collective-permute-start(f32[2,1,4096]{2,1,0:T(1,128)S(1)} %get-tuple-element.35), channel_id=1, source_target_pairs={{0,1},{1,2},{2,3},{3,4},{4,5},{5,6},{6,7},{7,8},{8,9},{9,10},{10,1... | collective-permute-start | bytes 98312 | tf_op jit(solution)/shard_map/ppermute | solution.py:20
  136.1 8.8 %collective-permute-start.6 = (f32[2,1,4096]{2,1,0:T(1,128)S(1)}, f32[2,1,4096]{2,1,0:T(1,128)S(1)}, u32[]{:S(2)}, u32[]{:S(2)}) collective-permute-start(f32[2,1,4096]{2,1,0:T(1,128)S(1)} %get-tuple-element.36), channel_id=1, source_target_pairs={{1,0},{2,1},{3,2},{4,3},{5,4},{6,5},{7,6},{8,7},{9,8},{10,9},{11,1... | collective-permute-start | bytes 98312 | tf_op jit(solution)/shard_map/ppermute | solution.py:21
  146.7 4.3 %collective-permute-start.7 = (f32[2,1,4096]{2,1,0:T(1,128)S(1)}, f32[2,1,4096]{2,1,0:T(1,128)S(1)}, u32[]{:S(2)}, u32[]{:S(2)}) collective-permute-start(f32[2,1,4096]{2,1,0:T(1,128)S(1)} %get-tuple-element.33), channel_id=1, source_target_pairs={{0,1},{1,2},{2,3},{3,4},{4,5},{5,6},{6,7},{7,8},{8,9},{9,10},{10,1... | collective-permute-start | bytes 98312 | tf_op jit(solution)/shard_map/ppermute | solution.py:20
  148.6 8.8 %collective-permute-start.8 = (f32[2,1,4096]{2,1,0:T(1,128)S(1)}, f32[2,1,4096]{2,1,0:T(1,128)S(1)}, u32[]{:S(2)}, u32[]{:S(2)}) collective-permute-start(f32[2,1,4096]{2,1,0:T(1,128)S(1)} %get-tuple-element.34), channel_id=1, source_target_pairs={{1,0},{2,1},{3,2},{4,3},{5,4},{6,5},{7,6},{8,7},{9,8},{10,9},{11,1... | collective-permute-start | bytes 98312 | tf_op jit(solution)/shard_map/ppermute | solution.py:21
  159.3 4.5 %collective-permute-start.9 = (f32[2,1,4096]{2,1,0:T(1,128)S(1)}, f32[2,1,4096]{2,1,0:T(1,128)S(1)}, u32[]{:S(2)}, u32[]{:S(2)}) collective-permute-start(f32[2,1,4096]{2,1,0:T(1,128)S(1)} %get-tuple-element.31), channel_id=1, source_target_pairs={{0,1},{1,2},{2,3},{3,4},{4,5},{5,6},{6,7},{7,8},{8,9},{9,10},{10,1... | collective-permute-start | bytes 98312 | tf_op jit(solution)/shard_map/ppermute | solution.py:20
  161.3 8.8 %collective-permute-start.10 = (f32[2,1,4096]{2,1,0:T(1,128)S(1)}, f32[2,1,4096]{2,1,0:T(1,128)S(1)}, u32[]{:S(2)}, u32[]{:S(2)}) collective-permute-start(f32[2,1,4096]{2,1,0:T(1,128)S(1)} %get-tuple-element.32), channel_id=1, source_target_pairs={{1,0},{2,1},{3,2},{4,3},{5,4},{6,5},{7,6},{8,7},{9,8},{10,9},{11,1... | collective-permute-start | bytes 98312 | tf_op jit(solution)/shard_map/ppermute | solution.py:21
  172.1 4.3 %collective-permute-start.11 = (f32[2,1,4096]{2,1,0:T(1,128)S(1)}, f32[2,1,4096]{2,1,0:T(1,128)S(1)}, u32[]{:S(2)}, u32[]{:S(2)}) collective-permute-start(f32[2,1,4096]{2,1,0:T(1,128)S(1)} %get-tuple-element.29), channel_id=1, source_target_pairs={{0,1},{1,2},{2,3},{3,4},{4,5},{5,6},{6,7},{7,8},{8,9},{9,10},{10,1... | collective-permute-start | bytes 98312 | tf_op jit(solution)/shard_map/ppermute | solution.py:20
  174.0 8.8 %collective-permute-start.12 = (f32[2,1,4096]{2,1,0:T(1,128)S(1)}, f32[2,1,4096]{2,1,0:T(1,128)S(1)}, u32[]{:S(2)}, u32[]{:S(2)}) collective-permute-start(f32[2,1,4096]{2,1,0:T(1,128)S(1)} %get-tuple-element.30), channel_id=1, source_target_pairs={{1,0},{2,1},{3,2},{4,3},{5,4},{6,5},{7,6},{8,7},{9,8},{10,9},{11,1... | collective-permute-start | bytes 98312 | tf_op jit(solution)/shard_map/ppermute | solution.py:21
  185.0 4.3 %collective-permute-start.13 = (f32[2,1,4096]{2,1,0:T(1,128)S(1)}, f32[2,1,4096]{2,1,0:T(1,128)S(1)}, u32[]{:S(2)}, u32[]{:S(2)}) collective-permute-start(f32[2,1,4096]{2,1,0:T(1,128)S(1)} %get-tuple-element.27), channel_id=1, source_target_pairs={{0,1},{1,2},{2,3},{3,4},{4,5},{5,6},{6,7},{7,8},{8,9},{9,10},{10,1... | collective-permute-start | bytes 98312 | tf_op jit(solution)/shard_map/ppermute | solution.py:20
  186.9 8.8 %collective-permute-start.14 = (f32[2,1,4096]{2,1,0:T(1,128)S(1)}, f32[2,1,4096]{2,1,0:T(1,128)S(1)}, u32[]{:S(2)}, u32[]{:S(2)}) collective-permute-start(f32[2,1,4096]{2,1,0:T(1,128)S(1)} %get-tuple-element.28), channel_id=1, source_target_pairs={{1,0},{2,1},{3,2},{4,3},{5,4},{6,5},{7,6},{8,7},{9,8},{10,9},{11,1... | collective-permute-start | bytes 98312 | tf_op jit(solution)/shard_map/ppermute | solution.py:21
  198.0 4.3 %collective-permute-start.15 = (f32[2,1,4096]{2,1,0:T(1,128)S(1)}, f32[2,1,4096]{2,1,0:T(1,128)S(1)}, u32[]{:S(2)}, u32[]{:S(2)}) collective-permute-start(f32[2,1,4096]{2,1,0:T(1,128)S(1)} %get-tuple-element.25), channel_id=1, source_target_pairs={{0,1},{1,2},{2,3},{3,4},{4,5},{5,6},{6,7},{7,8},{8,9},{9,10},{10,1... | collective-permute-start | bytes 98312 | tf_op jit(solution)/shard_map/ppermute | solution.py:20
  199.9 8.8 %collective-permute-start.16 = (f32[2,1,4096]{2,1,0:T(1,128)S(1)}, f32[2,1,4096]{2,1,0:T(1,128)S(1)}, u32[]{:S(2)}, u32[]{:S(2)}) collective-permute-start(f32[2,1,4096]{2,1,0:T(1,128)S(1)} %get-tuple-element.26), channel_id=1, source_target_pairs={{1,0},{2,1},{3,2},{4,3},{5,4},{6,5},{7,6},{8,7},{9,8},{10,9},{11,1... | collective-permute-start | bytes 98312 | tf_op jit(solution)/shard_map/ppermute | solution.py:21
  211.1 4.6 %collective-permute-start.17 = (f32[2,1,4096]{2,1,0:T(1,128)S(1)}, f32[2,1,4096]{2,1,0:T(1,128)S(1)}, u32[]{:S(2)}, u32[]{:S(2)}) collective-permute-start(f32[2,1,4096]{2,1,0:T(1,128)S(1)} %get-tuple-element.23), channel_id=1, source_target_pairs={{0,1},{1,2},{2,3},{3,4},{4,5},{5,6},{6,7},{7,8},{8,9},{9,10},{10,1... | collective-permute-start | bytes 98312 | tf_op jit(solution)/shard_map/ppermute | solution.py:20
  213.0 8.8 %collective-permute-start.18 = (f32[2,1,4096]{2,1,0:T(1,128)S(1)}, f32[2,1,4096]{2,1,0:T(1,128)S(1)}, u32[]{:S(2)}, u32[]{:S(2)}) collective-permute-start(f32[2,1,4096]{2,1,0:T(1,128)S(1)} %get-tuple-element.24), channel_id=1, source_target_pairs={{1,0},{2,1},{3,2},{4,3},{5,4},{6,5},{7,6},{8,7},{9,8},{10,9},{11,1... | collective-permute-start | bytes 98312 | tf_op jit(solution)/shard_map/ppermute | solution.py:21
where the time goes:
time: 322 us; the launch traced here: 321 us
  blocking collectives  135 us (42%)
  waiting for transfers between devices  95.3 us (30%)
  starting transfers between devices  57.8 us (18%)
  other arithmetic  21.6 us (7%)
  local copies, waits for them, and re-layouts  6.15 us (2%)
  matrix products  3.58 us (1%)
    all_to_all x1, blocking collectives, per_device(): lax.all_to_all(solved[:, None], 'tm', split_axis=2, concat_axis=1, tiled=...  54.5 us
    ppermute x9, waiting for transfers between devices, with_halo(): after = lax.ppermute(leading, axis, down)  51.9 us
    all_to_all x1, blocking collectives, per_device(): lax.all_to_all(scaled[None], 'tm', split_axis=1, concat_axis=0, tiled=True)  44.5 us
    all_to_all x1, waiting for transfers between devices, per_device(): lax.all_to_all(jnp.stack([spec_real, spec_imag]), 'tm', split_axis=1, con...  43.3 us
    all_to_all x1, blocking collectives, per_device(): lax.all_to_all(inverse, 'tm', split_axis=0, concat_axis=1, tiled=True)[0]  36.5 us
    ppermute x9, starting transfers between devices, with_halo(): before = lax.ppermute(last, axis, up)  26.7 us
    ppermute x9, starting transfers between devices, with_halo(): after = lax.ppermute(leading, axis, down)  21.7 us
    add x8, other arithmetic, relax_sweep(): combined = spectrum + neighbours(extended, face_set)  10 us
  transfers between devices with their start and end apart: 20, of which 9 were waited for; matrix products, arithmetic and copies ran while one was open for 1% of the time, Pallas kernels for 0%

commit v1 on v0

v1 whole, which is shorter than its diff:
```python
import functools

import jax
import jax.numpy as jnp
from jax import lax
from jax.experimental import pallas as pl
from jax.experimental.pallas import tpu as pltpu
from jax.sharding import PartitionSpec as P

ALPHA = 0.05
OMEGA = 0.8
SWEEPS = 8
LANES = 128
RIM = 8
MESH = pl.DeviceIdType.MESH
F32 = jnp.float32


def lane_index(shape):
    return lax.broadcasted_iota(jnp.int32, shape, len(shape) - 1)


def beside(own, other):
    lane = lane_index(own.shape)
    axis = own.ndim - 1
    left = jnp.where(lane == 0, pltpu.roll(other, 1, axis), pltpu.roll(own, 1, axis))
    right = jnp.where(
        lane == LANES - 1, pltpu.roll(other, LANES - 1, axis), pltpu.roll(own, LANES - 1, axis)
    )
    return left, right


def flag(condition):
    return jnp.where(condition, 1.0, 0.0).astype(F32)


def kernel(
    T, S, Z, R,
    u_hbm, s_hbm, c_hbm, out_hbm,
    u, s, c,
    edge_out, edge_in, rim_out, rim_in,
    from_prev, from_next, stage,
    xa, xb, wa, wb, qa, qb,
    pack, pack_left, pack_right,
    ca, cb, ka, kb,
    load_sem, edge_send, edge_recv, rim_send, rim_recv,
    up_send, down_send, prev_recv, next_recv,
    fwd_send, fwd_recv, row_send, row_recv, col_send, col_recv,
    back_send, back_recv,
):
    n, sp = lax.axis_index("tm"), lax.axis_index("space")
    XL = T // Z
    half = Z // 2
    z = lax.rem(n, Z)
    nxt, prv = lax.rem(n + 1, T), lax.rem(n + T - 1, T)
    below, above = lax.rem(sp + 1, S), lax.rem(sp + S - 1, S)
    has_above, has_below = flag(sp > 0), flag(sp < S - 1)
    E = R + 2 * RIM
    base = RIM
    own = base + RIM

    loads = [
        pltpu.make_async_copy(a, b, load_sem.at[i])
        for i, (a, b) in enumerate(((u_hbm, u), (c_hbm, c), (s_hbm, s)))
    ]
    for load in loads:
        load.start()

    barrier = pltpu.get_barrier_semaphore()

    def greet(i, carry):
        pl.semaphore_signal(
            barrier, inc=1, device_id=(lax.rem(n + i, T), sp), device_id_type=MESH
        )
        return carry

    lax.fori_loop(1, T, greet, 0)
    for row in (above, below):
        for step in (prv, n, nxt):
            pl.semaphore_signal(barrier, inc=1, device_id=(step, row), device_id_type=MESH)
    loads[0].wait()
    loads[1].wait()
    for side, row in ((0, 0), (1, R - 1)):
        edge_out[side, 0:1, :] = u[row : row + 1, :]
        edge_out[side, 1:2, :] = c[row : row + 1, :]
    tiles = [pl.ds(pl.multiple_of(k * LANES, LANES), LANES) for k in (prv, n, nxt)]
    for place, tile in enumerate(tiles):
        rim_out[0, place] = c[0:RIM, tile]
        rim_out[1, place] = c[R - RIM : R, tile]
    pl.semaphore_wait(barrier, T - 1 + 6)

    sides = []
    for side, row in ((0, above), (1, below)):
        for src, dst, send, recv in (
            (edge_out, edge_in, edge_send, edge_recv),
            (rim_out, rim_in, rim_send, rim_recv),
        ):
            sides.append(
                pltpu.make_async_remote_copy(
                    src_ref=src.at[side],
                    dst_ref=dst.at[1 - side],
                    send_sem=send.at[side],
                    recv_sem=recv.at[1 - side],
                    device_id=(n, row),
                    device_id_type=MESH,
                )
            )
    for copy in sides:
        copy.start()

    def columns(k):
        return pl.ds(pl.multiple_of(k * LANES, LANES), LANES)

    def place(j):
        return half - 1 - j // XL, lax.rem(j, XL)

    def block_ahead(j, start):
        away, row = place(j)
        return row * Z + lax.rem(start + away, Z)

    def block_behind(j, start):
        away, row = place(j)
        return row * Z + lax.rem(start + Z - away, Z)

    def iterate_copy(j):
        return pltpu.make_async_remote_copy(
            src_ref=u.at[:, columns(block_ahead(j, lax.rem(z + 1, Z)))],
            dst_ref=from_prev.at[j],
            send_sem=up_send,
            recv_sem=prev_recv.at[j],
            device_id=(nxt, sp),
            device_id_type=MESH,
        )

    def partial_copy(j):
        return pltpu.make_async_remote_copy(
            src_ref=stage.at[j],
            dst_ref=from_next.at[j],
            send_sem=down_send,
            recv_sem=next_recv.at[j],
            device_id=(prv, sp),
            device_id_type=MESH,
        )

    def send_iterate(j, carry):
        iterate_copy(j).start()
        return carry

    lax.fori_loop(0, T // 2, send_iterate, 0)

    loads[2].wait()
    for copy in sides[0::2]:
        copy.wait_recv()

    row_of = lax.broadcasted_iota(jnp.int32, (R, LANES), 0)

    def partial(k):
        here = columns(k)
        before, after = columns(lax.rem(k + T - 1, T)), columns(lax.rem(k + 1, T))
        inner_left, inner_right = flag(k > 0), flag(k < T - 1)
        lane = lane_index((R, LANES))

        def around(ref, which):
            middle = ref[:, here]
            left = jnp.where(
                lane == 0,
                pltpu.roll(ref[:, before], 1, 1) * inner_left,
                pltpu.roll(middle, 1, 1),
            )
            right = jnp.where(
                lane == LANES - 1,
                pltpu.roll(ref[:, after], LANES - 1, 1) * inner_right,
                pltpu.roll(middle, LANES - 1, 1),
            )
            top = edge_in[0, which : which + 1, here] * has_above
            bottom = edge_in[1, which : which + 1, here] * has_below
            up = jnp.where(row_of == 0, top, pltpu.roll(middle, 1, 0))
            down = jnp.where(row_of == R - 1, bottom, pltpu.roll(middle, R - 1, 0))
            return middle, (up, down, left, right)

        value, value_near = around(u, 0)
        cond, cond_near = around(c, 1)
        total = s[:, here] - value
        for near_value, near_cond in zip(value_near, cond_near):
            total = total + 0.5 * (cond + near_cond) * (near_value - value)
        return total

    def send_partial(j, carry):
        stage[j] = partial(block_behind(j, lax.rem(z + Z - 1, Z)))
        partial_copy(j).start()
        return carry

    lax.fori_loop(0, T // 2, send_partial, 0)

    def forward_copy(src, step, k):
        return pltpu.make_async_remote_copy(
            src_ref=src,
            dst_ref=xa.at[step, pl.ds(own, R), :],
            send_sem=fwd_send,
            recv_sem=fwd_recv.at[step],
            device_id=(k, sp),
            device_id_type=MESH,
        )

    def forward(src, step, k):
        @pl.when(k != n)
        def _():
            forward_copy(src, step, k).start()

        @pl.when(k == n)
        def _():
            pltpu.make_async_copy(
                src, xa.at[step, pl.ds(own, R), :], fwd_recv.at[step]
            ).start()

    is_first, is_last = flag(n > 0), flag(n < T - 1)

    def send_residuals(j, carry):
        partial_copy(j).wait_recv()
        k = block_behind(j, z)
        from_next[j] = from_next[j] + u[:, columns(k)] * is_last
        forward(from_next.at[j], nxt, k)
        iterate_copy(j).wait_recv()
        k = block_ahead(j, z)
        from_prev[j] = from_prev[j] * is_first + partial(k)
        forward(from_prev.at[j], n, k)
        return carry

    lax.fori_loop(0, T // 2, send_residuals, 0)

    for copy in sides[1::2]:
        copy.wait_recv()
    lane_e = lane_index((E, LANES))
    right_of, left_of = flag(n < T - 1), flag(n > 0)

    def tile_b(left, right):
        narrow = lane_index(left.shape)
        return jnp.where(narrow < LANES // 2, right * right_of, left * left_of)

    for ref, pick in (
        (ca, lambda parts: parts[1]),
        (cb, lambda parts: tile_b(parts[0], parts[2])),
    ):
        ref[base : base + RIM, :] = pick([rim_in[0, i] for i in range(3)]) * has_above
        ref[own : own + R, :] = pick([c[:, tile] for tile in tiles])
        ref[own + R : own + R + RIM, :] = pick([rim_in[1, i] for i in range(3)]) * has_below

    grid_row = sp * R - RIM + lax.broadcasted_iota(jnp.int32, (E, LANES), 0)
    row_ok = jnp.where(grid_row >= 0, 1.0, 0.0) * jnp.where(grid_row < S * R, 1.0, 0.0)
    col_ok = jnp.where(lane_e < LANES // 2, right_of, left_of)
    for ref, other, out, ok in ((ca, cb, ka, row_ok), (cb, ca, kb, row_ok * col_ok)):
        middle = ref[base : base + E, :]
        left, right = beside(middle, other[base : base + E, :])
        up, down = ref[base - 1 : base + E - 1, :], ref[base + 1 : base + E + 1, :]
        faces = [0.5 * (middle + near) for near in (up, down, left, right)]
        g = 1.0 / (1.0 + (faces[0] + faces[1] + faces[2] + faces[3]))
        for i, face in enumerate(faces):
            out[i] = jnp.where(ok > 0.0, OMEGA * g * face, 0.0)
        out[4] = g
        power = g
        count = 1
        while count < T:
            power = power * power
            count *= 2
        out[5] = ALPHA / (1.0 - ALPHA * power)
        out[6] = jnp.where(ok > 0.0, OMEGA * g, 0.0)

    def wait_forward(step, carry):
        forward_copy(xa.at[step, pl.ds(own, R), :], step, nxt).wait_recv()
        return carry

    lax.fori_loop(0, T, wait_forward, 0)

    row_copies = []
    for side, src, dst, row in (
        (0, own, own + R, above),
        (1, own + R - RIM, base, below),
    ):
        row_copies.append(
            pltpu.make_async_remote_copy(
                src_ref=xa.at[:, pl.ds(src, RIM), :],
                dst_ref=xa.at[:, pl.ds(dst, RIM), :],
                send_sem=row_send.at[side],
                recv_sem=row_recv.at[1 - side],
                device_id=(n, row),
                device_id_type=MESH,
            )
        )
    for copy in row_copies:
        copy.start()

    GROUPS = T // 8
    RG = R // 8
    lane_8 = lane_index((8, LANES))

    def pack_group(group, carry):
        for i in range(RG):
            total = jnp.zeros((8, LANES), F32)
            for j in range(8):
                rolled = pltpu.roll(xa[group * 8 + j, own + 8 * i : own + 8 * i + 8, :], 16 * j + 8, 1)
                total = jnp.where(lane_8 // 16 == j, rolled, total)
            pack[i, group] = total
        return carry

    lax.fori_loop(0, GROUPS, pack_group, 0)

    col_copies = []
    for side, (ref, step) in enumerate(((pack_left, nxt), (pack_right, prv))):
        for part, (src, dst, row) in enumerate((
            (pack, ref.at[pl.ds(1, RG)], sp),
            (pack.at[pl.ds(0, 1)], ref.at[pl.ds(RG + 1, 1)], above),
            (pack.at[pl.ds(RG - 1, 1)], ref.at[pl.ds(0, 1)], below),
        )):
            col_copies.append(
                pltpu.make_async_remote_copy(
                    src_ref=src,
                    dst_ref=dst,
                    send_sem=col_send.at[side * 3 + part],
                    recv_sem=col_recv.at[side * 3 + part],
                    device_id=(step, row),
                    device_id_type=MESH,
                )
            )
    for copy in col_copies:
        copy.start()
    for copy in col_copies:
        copy.wait_recv()

    def unpack_group(group, carry):
        for i in range(RG + 2):
            merged = jnp.where(
                lax.rem(lane_8, 16) < 8, pack_left[i, group], pack_right[i, group]
            )
            for j in range(8):
                xb[group * 8 + j, base + 8 * i : base + 8 * i + 8, :] = pltpu.roll(
                    merged, LANES - 8 - 16 * j, 1
                )
        return carry

    lax.fori_loop(0, GROUPS, unpack_group, 0)
    for copy in row_copies:
        copy.wait()

    BLOCK = 16
    UNROLL = 8

    def over_time(body, carry):
        def step(i, carry):
            for j in range(UNROLL):
                carry = body(i * UNROLL + j, carry)
            return carry

        return lax.fori_loop(0, T // UNROLL, step, carry)

    zero = jnp.zeros((BLOCK, LANES), F32)

    def wrap(first, dsts, coeffs, last):
        rows = pl.ds(base + first, BLOCK)
        gains = [k[4, first : first + BLOCK, :] for k in coeffs]
        start = tuple(
            value * k[5, first : first + BLOCK, :] for value, k in zip(last, coeffs)
        )

        def body(t, carry):
            new = []
            for dst, gain, value in zip(dsts, gains, carry):
                value = gain * value
                dst[t, rows, :] = dst[t, rows, :] + value
                new.append(value)
            return tuple(new)

        over_time(body, start)

    def first_sweep(first):
        rows = pl.ds(base + first, BLOCK)
        q_rows = pl.ds(first, BLOCK)
        for x, w, q, k in ((xa, wa, qa, ka), (xb, wb, qb, kb)):
            gain, weight = k[4, first : first + BLOCK, :], k[6, first : first + BLOCK, :]
            ok = weight > 0.0

            def body(t, carry):
                scaled = jnp.where(ok, weight * x[t, rows, :], 0.0)
                q[t, q_rows, :] = scaled
                value = scaled + gain * carry
                w[t, rows, :] = value
                return value

            last = over_time(body, zero)
            wrap(first, (w,), (k,), (last,))

    def sweep(first, src_a, src_b, dst_a, dst_b, both):
        rows = pl.ds(base + first, BLOCK)
        rows_up, rows_down = pl.ds(base + first - 1, BLOCK), pl.ds(base + first + 1, BLOCK)
        q_rows = pl.ds(first, BLOCK)
        kept = (ka, kb) if both else (ka,)
        coeffs = [[k[i, first : first + BLOCK, :] for i in range(5)] for k in kept]

        def body(t, carry):
            a, b = src_a[t, rows, :], src_b[t, rows, :]
            new = []
            for src, dst, q, mine, other, k, value in zip(
                (src_a, src_b), (dst_a, dst_b), (qa, qb), (a, b), (b, a), coeffs, carry
            ):
                left, right = beside(mine, other)
                near = k[0] * src[t, rows_up, :] + k[1] * src[t, rows_down, :]
                near = near + (k[2] * left + k[3] * right)
                value = (q[t, q_rows, :] + near) + k[4] * value
                dst[t, rows, :] = (1.0 - OMEGA) * mine + value
                new.append(value)
            return tuple(new)

        last = over_time(body, (zero,) * len(kept))
        wrap(first, (dst_a, dst_b)[: len(kept)], kept, last)

    for first in range(0, E, BLOCK):
        first_sweep(first)

    def two_sweeps(i, carry):
        for first in range(0, E, BLOCK):
            sweep(first, wa, wb, xa, xb, True)
        for first in range(0, E, BLOCK):
            sweep(first, xa, xb, wa, wb, True)
        return carry

    lax.fori_loop(0, (SWEEPS - 2) // 2, two_sweeps, 0)
    for first in range(RIM, RIM + R, BLOCK):
        sweep(first, wa, wb, xa, xb, False)

    def back_copy(step, block):
        return pltpu.make_async_remote_copy(
            src_ref=xa.at[step, pl.ds(own, R), :],
            dst_ref=out_hbm.at[:, columns(block)],
            send_sem=back_send,
            recv_sem=back_recv.at[block],
            device_id=(step, sp),
            device_id_type=MESH,
        )

    def send_back(j, carry):
        m = j // XL
        away = half - (m + 1) // 2
        toward = jnp.where(lax.rem(m, 2) == 1, away, Z - away)
        step = lax.rem(j, XL) * Z + lax.rem(z + toward, Z)

        @pl.when(step != n)
        def _():
            back_copy(step, n).start()

        @pl.when(step == n)
        def _():
            pltpu.make_async_copy(
                xa.at[step, pl.ds(own, R), :], out_hbm.at[:, columns(n)], back_recv.at[n]
            ).start()

        return carry

    lax.fori_loop(0, T, send_back, 0)

    for copy in sides:
        copy.wait_send()
    for copy in col_copies:
        copy.wait_send()
    pltpu.make_async_copy(from_prev, from_prev, up_send).wait()
    pltpu.make_async_copy(stage, stage, down_send).wait()
    sent = xa.at[pl.ds(0, T - 2), pl.ds(own, R), :]
    pltpu.make_async_copy(sent, sent, fwd_send).wait()
    sent = xa.at[pl.ds(0, T - 1), pl.ds(own, R), :]
    pltpu.make_async_copy(sent, sent, back_send).wait()

    def wait_back(block, carry):
        back_copy(nxt, block).wait_recv()
        return carry

    lax.fori_loop(0, T, wait_back, 0)


def per_device(iterate, source, conduct):
    T, S = lax.axis_size("tm"), lax.axis_size("space")
    R, NC = conduct.shape
    Z = T // 2
    E = R + 2 * RIM
    padded = E + 16
    dma = pltpu.SemaphoreType.DMA
    vmem = lambda *shape: pltpu.VMEM(shape, F32)
    any_space = pl.BlockSpec(memory_space=pl.ANY)
    correction = pl.pallas_call(
        functools.partial(kernel, T, S, Z, R),
        out_shape=jax.ShapeDtypeStruct((R, NC), F32),
        in_specs=[any_space] * 3,
        out_specs=any_space,
        scratch_shapes=[
            vmem(R, NC), vmem(R, NC), vmem(R, NC),
            vmem(2, 2, NC), vmem(2, 2, NC), vmem(2, 3, RIM, LANES), vmem(2, 3, RIM, LANES),
            vmem(T // 2, R, LANES), vmem(T // 2, R, LANES), vmem(T // 2, R, LANES),
            vmem(T, padded, LANES), vmem(T, padded, LANES),
            vmem(T, padded, LANES), vmem(T, padded, LANES),
            vmem(T, E, LANES), vmem(T, E, LANES),
            vmem(R // 8, T // 8, 8, LANES),
            vmem(R // 8 + 2, T // 8, 8, LANES), vmem(R // 8 + 2, T // 8, 8, LANES),
            vmem(padded, LANES), vmem(padded, LANES),
            vmem(7, E, LANES), vmem(7, E, LANES),
            dma((3,)), dma((2,)), dma((2,)), dma((2,)), dma((2,)),
            dma, dma, dma((T // 2,)), dma((T // 2,)),
            dma, dma((T,)), dma((2,)), dma((2,)), dma((6,)), dma((6,)),
            dma, dma((T,)),
        ],
        compiler_params=pltpu.CompilerParams(
            collective_id=0, has_side_effects=True, vmem_limit_bytes=32 * 1024 * 1024
        ),
    )(iterate[0], source[0], conduct)
    return iterate + correction[None]


def solution(mesh):
    return jax.shard_map(
        per_device,
        mesh=mesh,
        in_specs=(P("tm", "space", None), P("tm", "space", None), P("space", None)),
        out_specs=P("tm", "space", None),
        check_vma=False,
    )
```

time: 322 us -> 97.2 us (0.30)
  the two profiles are of different devices: /device:TPU:57 before, /device:TPU:6 now
where the time goes in v1:
time: 97.2 us; the launch traced here: 96.7 us
  Pallas kernels  92.7 us (95%)
  local copies, waits for them, and re-layouts  3.12 us (3%)
    pallas_call x1, Pallas kernels, per_device(): pl.pallas_call(functools.partial(kernel, T, S, Z, R), out_shape=jax.Shape...  92.7 us
    unnamed x6, local copies, waits for them, and re-layouts  3.12 us

profile of v1, /device:TPU:6, one launch (start us, length us, event | category | flops | bytes accessed | tf_op | source)
XLA Modules:
  0.0 96.7 jit_solution(6785403943247706130)
XLA Ops:
  0.0 0.0 copy-start
  0.0 1.0 %copy-done = f32[1,32,4096]{2,1,0:T(8,128)S(1)} copy-done((f32[1,32,4096]{2,1,0:T(8,128)S(1)}, f32[1,32,4096]{2,1,0:T(8,128)}, u32[]{:S(2)}) %copy-start) | copy-done | bytes 524312
  1.0 0.0 copy-start.1
  1.0 1.0 %copy-done.1 = f32[1,32,4096]{2,1,0:T(8,128)S(1)} copy-done((f32[1,32,4096]{2,1,0:T(8,128)S(1)}, f32[1,32,4096]{2,1,0:T(8,128)}, u32[]{:S(2)}) %copy-start.1) | copy-done | bytes 524312
  2.1 0.0 copy-start.2
  2.1 1.0 %copy-done.2 = f32[32,4096]{1,0:T(8,128)S(1)} copy-done((f32[32,4096]{1,0:T(8,128)S(1)}, f32[32,4096]{1,0:T(8,128)}, u32[]{:S(2)}) %copy-start.2) | copy-done | bytes 524312
  3.1 92.7 %shard_map.37 = f32[32,4096]{1,0:T(8,128)S(1)} custom-call(f32[32,4096]{1,0:T(8,128)S(1)} %bitcast.4, f32[32,4096]{1,0:T(8,128)S(1)} %bitcast.5, f32[32,4096]{1,0:T(8,128)S(1)} %copy-done.2), custom_call_target="tpu_custom_call" | custom-call | tf_op jit(solution)/shard_map/pallas_call | solution.py:486
  95.9 0.8 bitcast_add_fusion
Async XLA Ops:
  0.0 1.0 %copy-start = (f32[1,32,4096]{2,1,0:T(8,128)S(1)}, f32[1,32,4096]{2,1,0:T(8,128)}, u32[]{:S(2)}) copy-start(f32[1,32,4096]{2,1,0:T(8,128)} %param.3) | copy-start | bytes 1572868
  1.0 1.0 %copy-start.1 = (f32[1,32,4096]{2,1,0:T(8,128)S(1)}, f32[1,32,4096]{2,1,0:T(8,128)}, u32[]{:S(2)}) copy-start(f32[1,32,4096]{2,1,0:T(8,128)} %param.4) | copy-start | bytes 1572868
  2.1 1.0 %copy-start.2 = (f32[32,4096]{1,0:T(8,128)S(1)}, f32[32,4096]{1,0:T(8,128)}, u32[]{:S(2)}) copy-start(f32[32,4096]{1,0:T(8,128)} %c_hbm.1) | copy-start | bytes 1572868

commit v2 on v0

v2 whole, which is shorter than its diff:
```python
import functools

import jax
import jax.numpy as jnp
from jax import lax
from jax.experimental import pallas as pl
from jax.experimental.pallas import tpu as pltpu
from jax.sharding import PartitionSpec as P

ALPHA = 0.05
OMEGA = 0.8
SWEEPS = 8
LANES = 128
WIDTH = 64
RIM = 8
MESH = pl.DeviceIdType.MESH
F32 = jnp.float32


def lane_index(shape):
    return lax.broadcasted_iota(jnp.int32, shape, len(shape) - 1)


def roll(value, shift):
    shift = shift % LANES
    return pltpu.roll(value, shift, value.ndim - 1) if shift else value


def flag(condition):
    return jnp.where(condition, 1.0, 0.0).astype(F32)


def kernel(
    T, S, Z, R,
    u_hbm, s_hbm, c_hbm, out_hbm,
    u, s, c, out,
    edge_out, edge_in, rim_out, rim_in,
    u_stage, s_stage, from_prev, from_next,
    gathered, rows_out, rows_in, right_out, left_out, right_in, left_in,
    x_buf, w_buf, q_buf, cond_buf, coeff,
    back_out, back_in,
    load_sem, store_sem, edge_send, edge_recv, rim_send, rim_recv,
    u_send, s_send, prev_recv, next_recv,
    fwd_send, fwd_recv, row_send, row_recv, col_send, col_recv,
    back_send, back_recv,
):
    n, sp = lax.axis_index("tm"), lax.axis_index("space")
    XL = T // Z
    half = Z // 2
    z = lax.rem(n, Z)
    z_next, z_prev = lax.rem(z + 1, Z), lax.rem(z + Z - 1, Z)
    nxt, prv = lax.rem(n + 1, T), lax.rem(n + T - 1, T)
    below, above = lax.rem(sp + 1, S), lax.rem(sp + S - 1, S)
    has_above, has_below = flag(sp > 0), flag(sp < S - 1)
    H = R // 2
    E = R + 2 * RIM
    base = RIM
    own = base + RIM
    PAIRS = T // 2

    finish = []
    loads = []
    pieces = [(0, RIM), (R - RIM, RIM), (RIM, R - 2 * RIM)]
    for i, (a, b) in enumerate(((u_hbm, u), (c_hbm, c), (s_hbm, s))):
        loads.append([
            pltpu.make_async_copy(a.at[pl.ds(at, rows)], b.at[pl.ds(at, rows)], load_sem.at[i, q])
            for q, (at, rows) in enumerate(pieces)
        ])
    for group in ((0, 0), (0, 1), (1, 0), (1, 1), (0, 2), (1, 2), (2, 0), (2, 1), (2, 2)):
        loads[group[0]][group[1]].start()

    barrier = pltpu.get_barrier_semaphore()

    def greet(i, carry):
        pl.semaphore_signal(
            barrier, inc=1, device_id=(lax.rem(n + i, T), sp), device_id_type=MESH
        )
        return carry

    lax.fori_loop(1, T, greet, 0)
    for row in (above, below):
        pl.semaphore_signal(barrier, inc=1, device_id=(n, row), device_id_type=MESH)

    def columns(tile):
        return pl.ds(pl.multiple_of(tile * LANES, LANES), LANES)

    def remote(src, dst, send, recv, step, row):
        return pltpu.make_async_remote_copy(
            src_ref=src, dst_ref=dst, send_sem=send, recv_sem=recv,
            device_id=(step, row), device_id_type=MESH,
        )

    def pack(low, high, odd):
        lane = lane_index(low.shape)
        is_odd = jnp.zeros(low.shape, jnp.int32) + odd
        kept = jnp.where(is_odd == 1, high, low)
        moved = roll(jnp.where(is_odd == 1, low, high), WIDTH)
        return jnp.where(lane // WIDTH == is_odd, kept, moved)

    def conduct_tile(rows, half_index):
        block = half_index * T + n
        tile, odd = block // 2, lax.rem(block, 2)
        first = c[rows, columns(lax.rem(tile + odd, T))]
        second = c[rows, columns(lax.rem(tile + odd + T - 1, T))]
        lane = lane_index(first.shape)
        is_odd = jnp.zeros(first.shape, jnp.int32) + odd
        joined = jnp.where(lane < 96 - WIDTH * is_odd, first, second)
        placed = jnp.where(is_odd == 1, roll(joined, WIDTH), joined)
        right_ok, left_ok = flag(block < 2 * T - 1), flag(block > 0)
        keep = jnp.where(lane < WIDTH, 1.0, jnp.where(lane < 96, right_ok, left_ok))
        return jnp.where(keep > 0.0, placed, 0.0)

    for i, q in ((0, 0), (0, 1), (1, 0), (1, 1)):
        loads[i][q].wait()
    for side, row, rows in ((0, 0, slice(0, RIM)), (1, R - 1, slice(R - RIM, R))):
        edge_out[side, 0:1, :] = u[row : row + 1, :]
        edge_out[side, 1:2, :] = c[row : row + 1, :]
        for p in range(2):
            rim_out[side, p] = conduct_tile(rows, p)
    loads[0][2].wait()
    loads[1][2].wait()
    pl.semaphore_wait(barrier, T - 1 + 2)

    sides = []
    for src, dst, send, recv in (
        (edge_out, edge_in, edge_send, edge_recv),
        (rim_out, rim_in, rim_send, rim_recv),
    ):
        for side, row in ((0, above), (1, below)):
            sides.append(
                remote(src.at[side], dst.at[1 - side], send.at[side], recv.at[1 - side], n, row)
            )
    for copy in sides:
        copy.start()
        finish.append(copy.wait_send)

    def owner_ahead(j, start):
        away = half - 1 - j // XL
        return lax.rem(j, XL) * Z + lax.rem(start + away, Z)

    def owner_behind(j, start):
        away = half - 1 - j // XL
        return lax.rem(j, XL) * Z + lax.rem(start + Z - away, Z)

    def u_copy(p, j):
        return remote(
            u_stage.at[p, j], from_prev.at[p, j], u_send, prev_recv.at[p, j], nxt, sp
        )

    def s_copy(p, j):
        return remote(
            s_stage.at[p, j], from_next.at[p, j], s_send, next_recv.at[p, j], prv, sp
        )

    row_of = lax.broadcasted_iota(jnp.int32, (R, LANES), 0)
    lane_r = lane_index((R, LANES))

    def packed_iterate(p, k):
        here = columns((p * T + k) // 2)
        return pack(u[0:H, here], u[H:R, here], lax.rem(k, 2))

    def packed_partial(p, k):
        tile = (p * T + k) // 2
        here = columns(tile)
        before, after = columns(lax.rem(tile + T - 1, T)), columns(lax.rem(tile + 1, T))
        inner_left, inner_right = flag(tile > 0), flag(tile < T - 1)

        def around(ref, which):
            middle = ref[:, here]
            left = jnp.where(lane_r == 0, roll(ref[:, before], 1) * inner_left, roll(middle, 1))
            right = jnp.where(
                lane_r == LANES - 1, roll(ref[:, after], -1) * inner_right, roll(middle, -1)
            )
            top = edge_in[0, which : which + 1, here] * has_above
            bottom = edge_in[1, which : which + 1, here] * has_below
            up = jnp.where(row_of == 0, top, pltpu.roll(middle, 1, 0))
            down = jnp.where(row_of == R - 1, bottom, pltpu.roll(middle, R - 1, 0))
            return middle, (up, down, left, right)

        value, value_near = around(u, 0)
        cond, cond_near = around(c, 1)
        total = s[:, here] - value
        for near_value, near_cond in zip(value_near, cond_near):
            total = total + 0.5 * (cond + near_cond) * (near_value - value)
        return pack(total[0:H], total[H:R], lax.rem(k, 2))

    def over_blocks(p, owner, start, send):
        def step(j, carry):
            if p == 0:
                send(0, j, owner(j, start))
            else:
                k = owner(j, start)
                pl.when(k != 0)(lambda: send(1, j, k))
            return carry

        def early(j, carry):
            k = owner(j, start)
            pl.when(k == 0)(lambda: send(1, j, k))
            return carry

        if p == 0:
            lax.fori_loop(0, PAIRS, early, 0)
        lax.fori_loop(0, PAIRS, step, 0)

    def send_iterate(p, j, k):
        u_stage[p, j] = packed_iterate(p, k)
        u_copy(p, j).start()

    def send_partial(p, j, k):
        s_stage[p, j] = packed_partial(p, k)
        s_copy(p, j).start()

    over_blocks(0, owner_ahead, z_next, send_iterate)
    for load in loads[2]:
        load.wait()
    for copy in sides[0:2]:
        copy.wait_recv()
    over_blocks(0, owner_behind, z_prev, send_partial)
    finish.append(pltpu.make_async_copy(u_stage, u_stage, u_send).wait)
    finish.append(pltpu.make_async_copy(s_stage, s_stage, s_send).wait)

    def forward_copy(src, p, step, k):
        return remote(src, gathered.at[p, step], fwd_send, fwd_recv.at[p, step], k, sp)

    def forward(src, p, step, k):
        @pl.when(k != n)
        def _():
            forward_copy(src, p, step, k).start()

        @pl.when(k == n)
        def _():
            pltpu.make_async_copy(src, gathered.at[p, step], fwd_recv.at[p, step]).start()

    is_first, is_last = flag(n > 0), flag(n < T - 1)

    def forward_behind(p, j, k):
        s_copy(p, j).wait_recv()
        from_next[p, j] = from_next[p, j] + packed_iterate(p, k) * is_last
        forward(from_next.at[p, j], p, nxt, k)

    def forward_ahead(p, j, k):
        u_copy(p, j).wait_recv()
        from_prev[p, j] = from_prev[p, j] * is_first + packed_partial(p, k)
        forward(from_prev.at[p, j], p, n, k)

    def forward_some(p, start, stop, only=None):
        def both(j, carry):
            for owner, send in ((owner_behind, forward_behind), (owner_ahead, forward_ahead)):
                k = owner(j, z)
                if only is None:
                    send(p, j, k)
                else:
                    pl.when((k == 0) == only)(functools.partial(send, p, j, k))
            return carry

        lax.fori_loop(start, stop, both, 0)

    forward_some(1, 0, PAIRS, only=True)
    forward_some(0, 0, PAIRS)
    over_blocks(1, owner_ahead, z_next, send_iterate)
    over_blocks(1, owner_behind, z_prev, send_partial)
    sent = gathered.at[:, pl.ds(0, T - 2)]
    finish.append(pltpu.make_async_copy(sent, sent, fwd_send).wait)

    for copy in sides[2:4]:
        copy.wait_recv()
    lane_e = lane_index((E, LANES))
    grid_row = sp * R - RIM + lax.broadcasted_iota(jnp.int32, (E, LANES), 0)
    row_ok = jnp.where(grid_row >= 0, 1.0, 0.0) * jnp.where(grid_row < S * R, 1.0, 0.0)
    for p in range(2):
        cond_buf[base : base + RIM, :] = rim_in[0, p] * has_above
        cond_buf[own : own + R, :] = conduct_tile(slice(0, R), p)
        cond_buf[own + R : own + R + RIM, :] = rim_in[1, p] * has_below
        block = p * T + n
        right_ok, left_ok = flag(block < 2 * T - 1), flag(block > 0)
        ok = row_ok * jnp.where(lane_e < WIDTH, 1.0, jnp.where(lane_e < 96, right_ok, left_ok))
        middle = cond_buf[base : base + E, :]
        up, down = cond_buf[base - 1 : base + E - 1, :], cond_buf[base + 1 : base + E + 1, :]
        faces = [0.5 * (middle + near) for near in (up, down, roll(middle, 1), roll(middle, -1))]
        g = 1.0 / (1.0 + (faces[0] + faces[1] + faces[2] + faces[3]))
        for i, face in enumerate(faces):
            coeff[p, i] = jnp.where(ok > 0.0, OMEGA * g * face, 0.0)
        coeff[p, 4] = g
        power = g
        count = 1
        while count < T:
            power = power * power
            count *= 2
        coeff[p, 5] = ALPHA / (1.0 - ALPHA * power)
        coeff[p, 6] = jnp.where(ok > 0.0, OMEGA * g, 0.0)

    lane_8 = lane_index((8, LANES))
    segment, in_first = lane_8 // 16, lax.rem(lane_8, 16) < 8
    in_low = lane_8 < WIDTH

    def row_copies(p, group):
        return [
            remote(
                rows_out.at[p, side, group], rows_in.at[p, 1 - side, group],
                row_send, row_recv.at[p, 1 - side], n, row,
            )
            for side, row in ((0, above), (1, below))
        ]

    def send_rows(p):
        def pass_rows(group, carry):
            for j in range(8):
                forward_copy(gathered.at[p, 0], p, group * 8 + j, nxt).wait_recv()
            for j in range(4):
                step = group * 8 + 2 * j
                top, top_next = gathered[p, step, 0:8], gathered[p, step + 1, 0:8]
                rows_out[p, 0, group, j] = jnp.where(in_low, top, roll(top_next, WIDTH))
                bottom = gathered[p, step, H - 8 : H]
                bottom_next = gathered[p, step + 1, H - 8 : H]
                rows_out[p, 1, group, j] = jnp.where(in_low, roll(bottom, WIDTH), bottom_next)
            for copy in row_copies(p, group):
                copy.start()
            return carry

        lax.fori_loop(0, T // 8, pass_rows, 0)

    def packed_rows(p, group, j, i):
        if i < 2:
            return gathered[p, group * 8 + j, 8 * i : 8 * i + 8]
        down, up = rows_in[p, 1, group, j // 2], rows_in[p, 0, group, j // 2]
        if j % 2:
            return jnp.where(in_low, roll(down, WIDTH), up)
        return jnp.where(in_low, down, roll(up, WIDTH))

    def pack_edges(p):
        for side in range(2):
            whole = rows_in.at[p, side]
            pltpu.make_async_copy(whole, whole, row_recv.at[p, side]).wait()

        def pack_group(group, carry):
            for i in range(3):
                first = jnp.zeros((8, LANES), F32)
                second = first
                for j in range(8):
                    value = packed_rows(p, group, j, i)
                    first = jnp.where(segment == j, roll(value, 16 * j - 56), first)
                    second = jnp.where(segment == j, roll(value, 16 * j + 8), second)
                right_out[p, i, group] = jnp.where(in_first, first, roll(second, 8))
                left_out[p, i, group] = jnp.where(in_first, roll(first, -8), second)
            return carry

        lax.fori_loop(0, T // 8, pack_group, 0)

    def columns_copies(p):
        right = right_out.at[jnp.where(n == T - 1, 0, p)]
        left = left_out.at[jnp.where(n == 0, 1, p)]
        return (
            remote(right, right_in.at[p], col_send.at[p, 0], col_recv.at[p, 0], nxt, sp),
            remote(left, left_in.at[p], col_send.at[p, 1], col_recv.at[p, 1], prv, sp),
        )

    GROUPS = ((0, 2), (1, 3), (4, -1))

    def unpack(p):
        def unpack_group(group, carry):
            for i, (low, high) in enumerate(GROUPS):
                from_left, from_right = right_in[p, i, group], left_in[p, i, group]
                for j in range(8):
                    step = group * 8 + j
                    value = packed_rows(p, group, j, i)
                    for place, own_part, left_at, right_at in (
                        (low, value, 0, 8),
                        (high, roll(value, WIDTH), 8, 0),
                    ):
                        left = roll(from_left, 120 - 16 * j - left_at)
                        right = roll(from_right, 64 - 16 * j - right_at)
                        x_buf[step, own + 8 * place : own + 8 * place + 8, :] = jnp.where(
                            in_low, own_part, jnp.where(lane_8 < 96, right, left)
                        )
            return carry

        lax.fori_loop(0, T // 8, unpack_group, 0)

    def over_time(body, carry):
        for step in range(T):
            carry = body(step, carry)
        return carry

    def wrap(p, first, rows, dst, last):
        here = pl.ds(base + first, rows)
        gain = coeff[p, 4, first : first + rows, :]

        def body(t, carry):
            carry = gain * carry
            dst[t, here, :] = dst[t, here, :] + carry
            return carry

        over_time(body, last * coeff[p, 5, first : first + rows, :])

    def first_sweep(p, first, rows, src, dst):
        here, q_here = pl.ds(base + first, rows), pl.ds(first, rows)
        gain = coeff[p, 4, first : first + rows, :]
        weight = coeff[p, 6, first : first + rows, :]
        ok = weight > 0.0

        def body(t, carry):
            scaled = jnp.where(ok, weight * src[t, here, :], 0.0)
            q_buf[t, q_here, :] = scaled
            value = scaled + gain * carry
            dst[t, here, :] = value
            return value

        last = over_time(body, jnp.zeros((rows, LANES), F32))
        wrap(p, first, rows, dst, last)

    def sweep(p, first, rows, src, dst):
        here, q_here = pl.ds(base + first, rows), pl.ds(first, rows)
        here_up, here_down = pl.ds(base + first - 1, rows), pl.ds(base + first + 1, rows)
        k = [coeff[p, i, first : first + rows, :] for i in range(5)]

        def body(t, carry):
            mine = src[t, here, :]
            near = k[0] * src[t, here_up, :] + k[1] * src[t, here_down, :]
            near = near + (k[2] * roll(mine, 1) + k[3] * roll(mine, -1))
            value = (q_buf[t, q_here, :] + near) + k[4] * carry
            dst[t, here, :] = (1.0 - OMEGA) * mine + value
            return value

        last = over_time(body, jnp.zeros((rows, LANES), F32))
        wrap(p, first, rows, dst, last)

    def blocks_of(first, stop, rows):
        return [(at, min(rows, stop - at)) for at in range(first, stop, rows)]

    BLOCK = 24

    def solve(p):
        for first, rows in blocks_of(0, E, BLOCK):
            first_sweep(p, first, rows, x_buf, w_buf)

        def two_sweeps(i, carry):
            for first, rows in blocks_of(0, E, BLOCK):
                sweep(p, first, rows, w_buf, x_buf)
            for first, rows in blocks_of(0, E, BLOCK):
                sweep(p, first, rows, x_buf, w_buf)
            return carry

        lax.fori_loop(0, (SWEEPS - 2) // 2, two_sweeps, 0)
        for first, rows in blocks_of(RIM, RIM + R, 16):
            sweep(p, first, rows, w_buf, x_buf)

    def back_copy(p, step, k):
        return remote(back_out.at[p, step], back_in.at[p, k], back_send, back_recv.at[p, k], step, sp)

    def pack_back(p):
        lane = lane_index((H, LANES))

        def pack_step(step, carry):
            low, high = x_buf[step, own : own + H, :], x_buf[step, own + H : own + R, :]
            back_out[p, step] = jnp.where(lane < WIDTH, low, roll(high, WIDTH))
            return carry

        lax.fori_loop(0, T, pack_step, 0)

    def give_back(p, start, stop):
        def send(j, carry):
            m = j // XL
            away = half - (m + 1) // 2
            toward = jnp.where(lax.rem(m, 2) == 1, away, Z - away)
            step = lax.rem(j, XL) * Z + lax.rem(z + toward, Z)

            @pl.when(step != n)
            def _():
                back_copy(p, step, n).start()

            @pl.when(step == n)
            def _():
                pltpu.make_async_copy(
                    back_out.at[p, step], back_in.at[p, n], back_recv.at[p, n]
                ).start()

            return carry

        lax.fori_loop(start, stop, send, 0)

    def store_copy(tile):
        return pltpu.make_async_copy(out.at[:, columns(tile)], out_hbm.at[:, columns(tile)], store_sem)

    def update(p):
        lane = lane_index((H, LANES))

        def step(j, carry):
            m = j // XL
            away = half // 2 - (m + 1) // 2
            toward = jnp.where(lax.rem(m, 2) == 1, away, half - away)
            pair = lax.rem(j, XL) * half + lax.rem(z // 2 + toward, half)
            for k in (2 * pair, 2 * pair + 1):
                back_copy(p, nxt, k).wait_recv()
            even, odd = back_in[p, 2 * pair], back_in[p, 2 * pair + 1]
            tile = p * PAIRS + pair
            here = columns(tile)
            out[0:H, here] = u[0:H, here] + jnp.where(lane < WIDTH, even, roll(odd, WIDTH))
            out[H:R, here] = u[H:R, here] + jnp.where(lane < WIDTH, roll(even, WIDTH), odd)
            store_copy(tile).start()
            return carry

        lax.fori_loop(0, PAIRS, step, 0)

    def pass_columns(p):
        copies = columns_copies(p)
        for copy in copies:
            copy.start()
            finish.append(copy.wait_send)
        return copies

    send_rows(0)
    pl.when(n == 0)(lambda: send_rows(1))
    forward_some(1, 0, PAIRS // 2, only=False)
    pack_edges(0)
    pl.when(n == 0)(lambda: pack_edges(1))
    first_columns = pass_columns(0)
    forward_some(1, PAIRS // 2, PAIRS, only=False)
    for copy in first_columns:
        copy.wait_recv()
    unpack(0)
    solve(0)
    pack_back(0)

    pl.when(n != 0)(lambda: send_rows(1))
    give_back(0, 0, T // 4)
    pl.when(n != 0)(lambda: pack_edges(1))
    second_columns = pass_columns(1)
    give_back(0, T // 4, T // 2)
    for copy in second_columns:
        copy.wait_recv()
    unpack(1)
    give_back(0, T // 2, T)
    solve(1)
    pack_back(1)
    give_back(1, 0, T)
    update(0)
    update(1)
    whole = rows_in
    finish.append(pltpu.make_async_copy(whole, whole, row_send).wait)
    sent = back_out.at[:, pl.ds(0, T - 1)]
    finish.append(pltpu.make_async_copy(sent, sent, back_send).wait)
    finish.append(pltpu.make_async_copy(out, out, store_sem).wait)
    for wait in finish:
        wait()


def per_device(iterate, source, conduct):
    T, S = lax.axis_size("tm"), lax.axis_size("space")
    R, NC = conduct.shape
    Z = T // 2
    E = R + 2 * RIM
    dma = pltpu.SemaphoreType.DMA
    vmem = lambda *shape: pltpu.VMEM(shape, F32)
    block = (R // 2, LANES)
    group = (T // 8, 8, LANES)
    in_hbm = pl.BlockSpec(memory_space=pltpu.HBM)
    updated = pl.pallas_call(
        functools.partial(kernel, T, S, Z, R),
        out_shape=jax.ShapeDtypeStruct((R, NC), F32),
        in_specs=[in_hbm] * 3,
        out_specs=in_hbm,
        scratch_shapes=[
            vmem(R, NC), vmem(R, NC), vmem(R, NC), vmem(R, NC),
            vmem(2, 2, NC), vmem(2, 2, NC), vmem(2, 2, RIM, LANES), vmem(2, 2, RIM, LANES),
            vmem(2, T // 2, *block), vmem(2, T // 2, *block),
            vmem(2, T // 2, *block), vmem(2, T // 2, *block),
            vmem(2, T, *block), vmem(2, 2, T // 8, 4, RIM, LANES), vmem(2, 2, T // 8, 4, RIM, LANES),
            vmem(2, 3, *group), vmem(2, 3, *group), vmem(2, 3, *group), vmem(2, 3, *group),
            vmem(T, E + 16, LANES), vmem(T, E + 16, LANES), vmem(T, E, LANES),
            vmem(E + 16, LANES), vmem(2, 7, E, LANES),
            vmem(2, T, *block), vmem(2, T, *block),
            dma((3, 3)), dma, dma((2,)), dma((2,)), dma((2,)), dma((2,)),
            dma, dma, dma((2, T // 2)), dma((2, T // 2)),
            dma, dma((2, T)), dma, dma((2, 2)), dma((2, 2)), dma((2, 2)),
            dma, dma((2, T)),
        ],
        compiler_params=pltpu.CompilerParams(
            collective_id=0, has_side_effects=True, vmem_limit_bytes=60 * 1024 * 1024
        ),
    )(iterate[0], source[0], conduct)
    return updated[None]


def solution(mesh):
    return jax.shard_map(
        per_device,
        mesh=mesh,
        in_specs=(P("tm", "space", None), P("tm", "space", None), P("space", None)),
        out_specs=P("tm", "space", None),
        check_vma=False,
    )
```

time: 322 us -> 89.4 us (0.28)
  the two profiles are of different devices: /device:TPU:57 before, /device:TPU:6 now
where the time goes in v2:
time: 89.4 us; the launch traced here: 89.2 us
  Pallas kernels  87.3 us (98%)
  local copies, waits for them, and re-layouts  1.87 us (2%)
    pallas_call x1, Pallas kernels, per_device(): pl.pallas_call(functools.partial(kernel, T, S, Z, R), out_shape=jax.Shape...  87.3 us
    unnamed x1, local copies, waits for them, and re-layouts  1.87 us

profile of v2, /device:TPU:6, one launch (start us, length us, event | category | flops | bytes accessed | tf_op | source)
XLA Modules:
  0.0 89.2 jit_solution(1843620174646514650)
XLA Ops:
  0.0 87.3 %shard_map.37 = f32[32,4096]{1,0:T(8,128)} custom-call(f32[32,4096]{1,0:T(8,128)} %bitcast.4, f32[32,4096]{1,0:T(8,128)} %bitcast.5, f32[32,4096]{1,0:T(8,128)} %c_hbm.1), custom_call_target="tpu_custom_call" | custom-call | tf_op jit(solution)/shard_map/pallas_call | solution.py:557
  87.3 1.9 %copy.5 = f32[1,32,4096]{2,1,0:T(8,128)} copy(f32[1,32,4096]{2,1,0:T(8,128)} %bitcast.3) | data formatting | bytes 1048576

commit v3 on v2

--- a/solution.py
+++ b/solution.py
@@ -33,7 +33,7 @@
 def kernel(
     T, S, Z, R,
     u_hbm, s_hbm, c_hbm, out_hbm,
-    u, s, c, out,
+    u, s, c, out, part,
     edge_out, edge_in, rim_out, rim_in,
     u_stage, s_stage, from_prev, from_next,
     gathered, rows_out, rows_in, right_out, left_out, right_in, left_in,
@@ -41,7 +41,7 @@
     back_out, back_in,
     load_sem, store_sem, edge_send, edge_recv, rim_send, rim_recv,
     u_send, s_send, prev_recv, next_recv,
-    fwd_send, fwd_recv, row_send, row_recv, col_send, col_recv,
+    fwd_send, fwd_recv, halo_send, row_recv, col_send, col_recv, corner_recv,
     back_send, back_recv,
 ):
     n, sp = lax.axis_index("tm"), lax.axis_index("space")
@@ -57,6 +57,8 @@
     base = RIM
     own = base + RIM
     PAIRS = T // 2
+    PIECES = 4
+    PIECE = PAIRS // PIECES
 
     finish = []
     loads = []
@@ -78,8 +80,12 @@
         return carry
 
     lax.fori_loop(1, T, greet, 0)
-    for row in (above, below):
-        pl.semaphore_signal(barrier, inc=1, device_id=(n, row), device_id_type=MESH)
+    there = ((sp > 0, above), (sp < S - 1, below))
+    for exists, row in there:
+        @pl.when(exists)
+        def _(row=row):
+            for step in (prv, n, nxt):
+                pl.semaphore_signal(barrier, inc=1, device_id=(step, row), device_id_type=MESH)
 
     def columns(tile):
         return pl.ds(pl.multiple_of(tile * LANES, LANES), LANES)
@@ -119,20 +125,8 @@
             rim_out[side, p] = conduct_tile(rows, p)
     loads[0][2].wait()
     loads[1][2].wait()
-    pl.semaphore_wait(barrier, T - 1 + 2)
-
-    sides = []
-    for src, dst, send, recv in (
-        (edge_out, edge_in, edge_send, edge_recv),
-        (rim_out, rim_in, rim_send, rim_recv),
-    ):
-        for side, row in ((0, above), (1, below)):
-            sides.append(
-                remote(src.at[side], dst.at[1 - side], send.at[side], recv.at[1 - side], n, row)
-            )
-    for copy in sides:
-        copy.start()
-        finish.append(copy.wait_send)
+    for load in loads[2]:
+        load.wait()
 
     def owner_ahead(j, start):
         away = half - 1 - j // XL
@@ -142,80 +136,96 @@
         away = half - 1 - j // XL
         return lax.rem(j, XL) * Z + lax.rem(start + Z - away, Z)
 
-    def u_copy(p, j):
-        return remote(
-            u_stage.at[p, j], from_prev.at[p, j], u_send, prev_recv.at[p, j], nxt, sp
-        )
-
-    def s_copy(p, j):
-        return remote(
-            s_stage.at[p, j], from_next.at[p, j], s_send, next_recv.at[p, j], prv, sp
-        )
+    def packed(ref, p, k):
+        here = columns((p * T + k) // 2)
+        return pack(ref[0:H, here], ref[H:R, here], lax.rem(k, 2))
+
+    def stage_iterate(j, carry):
+        k = owner_ahead(j, z_next)
+        for p in range(2):
+            u_stage[p, j] = packed(u, p, k)
+        return carry
+
+    lax.fori_loop(0, PAIRS, stage_iterate, 0)
 
     row_of = lax.broadcasted_iota(jnp.int32, (R, LANES), 0)
     lane_r = lane_index((R, LANES))
 
-    def packed_iterate(p, k):
-        here = columns((p * T + k) // 2)
-        return pack(u[0:H, here], u[H:R, here], lax.rem(k, 2))
-
-    def packed_partial(p, k):
-        tile = (p * T + k) // 2
+    def partial(tile, carry):
         here = columns(tile)
         before, after = columns(lax.rem(tile + T - 1, T)), columns(lax.rem(tile + 1, T))
         inner_left, inner_right = flag(tile > 0), flag(tile < T - 1)
 
-        def around(ref, which):
+        def around(ref):
             middle = ref[:, here]
             left = jnp.where(lane_r == 0, roll(ref[:, before], 1) * inner_left, roll(middle, 1))
             right = jnp.where(
                 lane_r == LANES - 1, roll(ref[:, after], -1) * inner_right, roll(middle, -1)
             )
-            top = edge_in[0, which : which + 1, here] * has_above
-            bottom = edge_in[1, which : which + 1, here] * has_below
-            up = jnp.where(row_of == 0, top, pltpu.roll(middle, 1, 0))
-            down = jnp.where(row_of == R - 1, bottom, pltpu.roll(middle, R - 1, 0))
-            return middle, (up, down, left, right)
-
-        value, value_near = around(u, 0)
-        cond, cond_near = around(c, 1)
+            return middle, (left, right)
+
+        value, value_near = around(u)
+        cond, cond_near = around(c)
         total = s[:, here] - value
         for near_value, near_cond in zip(value_near, cond_near):
             total = total + 0.5 * (cond + near_cond) * (near_value - value)
-        return pack(total[0:H], total[H:R], lax.rem(k, 2))
-
-    def over_blocks(p, owner, start, send):
-        def step(j, carry):
-            if p == 0:
-                send(0, j, owner(j, start))
-            else:
-                k = owner(j, start)
-                pl.when(k != 0)(lambda: send(1, j, k))
-            return carry
-
-        def early(j, carry):
-            k = owner(j, start)
-            pl.when(k == 0)(lambda: send(1, j, k))
-            return carry
-
-        if p == 0:
-            lax.fori_loop(0, PAIRS, early, 0)
-        lax.fori_loop(0, PAIRS, step, 0)
-
-    def send_iterate(p, j, k):
-        u_stage[p, j] = packed_iterate(p, k)
-        u_copy(p, j).start()
-
-    def send_partial(p, j, k):
-        s_stage[p, j] = packed_partial(p, k)
-        s_copy(p, j).start()
-
-    over_blocks(0, owner_ahead, z_next, send_iterate)
-    for load in loads[2]:
-        load.wait()
-    for copy in sides[0:2]:
-        copy.wait_recv()
-    over_blocks(0, owner_behind, z_prev, send_partial)
+        flow = 0.5 * (cond + pltpu.roll(cond, 1, 0)) * (pltpu.roll(value, 1, 0) - value)
+        flow = jnp.where(row_of == 0, 0.0, flow)
+        part[:, here] = total + flow - pltpu.roll(flow, R - 1, 0)
+        return carry
+
+    lax.fori_loop(0, T, partial, 0)
+    beside = sum(jnp.where(exists, 1, 0) for exists, row in there)
+    pl.semaphore_wait(barrier, T - 1 + 3 * beside)
+
+    def when_there(side, action):
+        pl.when(there[side][0])(action)
+
+    def side_copies(src, dst, send, recv):
+        return [
+            remote(src.at[side], dst.at[1 - side], send.at[side], recv.at[side], n, there[side][1])
+            for side in range(2)
+        ]
+
+    edge_copies = side_copies(edge_out, edge_in, edge_send, edge_recv)
+    rim_copies = side_copies(rim_out, rim_in, rim_send, rim_recv)
+    for copies in (edge_copies, rim_copies):
+        for side in range(2):
+            when_there(side, copies[side].start)
+            finish.append(functools.partial(when_there, side, copies[side].wait_send))
+
+    def u_copy(p, piece):
+        some = pl.ds(piece * PIECE, PIECE)
+        return remote(
+            u_stage.at[p, some], from_prev.at[p, some], u_send, prev_recv.at[p, piece], nxt, sp
+        )
+
+    def s_copy(p, piece):
+        some = pl.ds(piece * PIECE, PIECE)
+        return remote(
+            s_stage.at[p, some], from_next.at[p, some], s_send, next_recv.at[p, piece], prv, sp
+        )
+
+    for p in range(2):
+        for piece in range(PIECES):
+            u_copy(p, piece).start()
+    for side, row, has in ((0, 0, has_above), (1, R - 1, has_below)):
+        when_there(side, edge_copies[1 - side].wait_recv)
+        value, cond = u[row : row + 1, :], c[row : row + 1, :]
+        value_near = jnp.where(has + jnp.zeros_like(value) > 0.0, edge_in[side, 0:1, :], 0.0)
+        cond_near = jnp.where(has + jnp.zeros_like(value) > 0.0, edge_in[side, 1:2, :], 0.0)
+        part[row : row + 1, :] = part[row : row + 1, :] + 0.5 * (cond + cond_near) * (
+            value_near - value
+        )
+    for p in range(2):
+        def send_partial(piece, carry, p=p):
+            for i in range(PIECE):
+                j = piece * PIECE + i
+                s_stage[p, j] = packed(part, p, owner_behind(j, z_prev))
+            s_copy(p, piece).start()
+            return carry
+
+        lax.fori_loop(0, PIECES, send_partial, 0)
     finish.append(pltpu.make_async_copy(u_stage, u_stage, u_send).wait)
     finish.append(pltpu.make_async_copy(s_stage, s_stage, s_send).wait)
 
@@ -233,44 +243,54 @@
 
     is_first, is_last = flag(n > 0), flag(n < T - 1)
 
-    def forward_behind(p, j, k):
-        s_copy(p, j).wait_recv()
-        from_next[p, j] = from_next[p, j] + packed_iterate(p, k) * is_last
-        forward(from_next.at[p, j], p, nxt, k)
-
-    def forward_ahead(p, j, k):
-        u_copy(p, j).wait_recv()
-        from_prev[p, j] = from_prev[p, j] * is_first + packed_partial(p, k)
-        forward(from_prev.at[p, j], p, n, k)
-
-    def forward_some(p, start, stop, only=None):
-        def both(j, carry):
-            for owner, send in ((owner_behind, forward_behind), (owner_ahead, forward_ahead)):
-                k = owner(j, z)
-                if only is None:
-                    send(p, j, k)
-                else:
-                    pl.when((k == 0) == only)(functools.partial(send, p, j, k))
-            return carry
-
-        lax.fori_loop(start, stop, both, 0)
-
-    forward_some(1, 0, PAIRS, only=True)
-    forward_some(0, 0, PAIRS)
-    over_blocks(1, owner_ahead, z_next, send_iterate)
-    over_blocks(1, owner_behind, z_prev, send_partial)
+    def forward_behind(p, j, k, prepare, start):
+        if prepare:
+            from_next[p, j] = from_next[p, j] + packed(u, p, k) * is_last
+        if start:
+            forward(from_next.at[p, j], p, nxt, k)
+
+    def forward_ahead(p, j, k, prepare, start):
+        if prepare:
+            from_prev[p, j] = from_prev[p, j] * is_first + packed(part, p, k)
+        if start:
+            forward(from_prev.at[p, j], p, n, k)
+
+    def forward_all(p, only=None, prepare=True, start=True, wait=True):
+        def one_piece(piece, carry):
+            if wait:
+                s_copy(p, piece).wait_recv()
+                u_copy(p, piece).wait_recv()
+            for i in range(PIECE):
+                j = piece * PIECE + i
+                for owner, send in (
+                    (owner_behind, forward_behind), (owner_ahead, forward_ahead)
+                ):
+                    k = owner(j, z)
+                    go = functools.partial(send, p, j, k, prepare, start)
+                    if only is None:
+                        go()
+                    else:
+                        pl.when((k == 0) == only)(go)
+            return carry
+
+        lax.fori_loop(0, PIECES, one_piece, 0)
+
+    forward_all(0)
+    forward_all(1, start=False)
+    forward_all(1, only=True, prepare=False, wait=False)
     sent = gathered.at[:, pl.ds(0, T - 2)]
     finish.append(pltpu.make_async_copy(sent, sent, fwd_send).wait)
 
-    for copy in sides[2:4]:
-        copy.wait_recv()
+    for side in range(2):
+        when_there(side, rim_copies[1 - side].wait_recv)
+    tile_zero = jnp.zeros((RIM, LANES), F32)
     lane_e = lane_index((E, LANES))
     grid_row = sp * R - RIM + lax.broadcasted_iota(jnp.int32, (E, LANES), 0)
     row_ok = jnp.where(grid_row >= 0, 1.0, 0.0) * jnp.where(grid_row < S * R, 1.0, 0.0)
     for p in range(2):
-        cond_buf[base : base + RIM, :] = rim_in[0, p] * has_above
+        cond_buf[base : base + RIM, :] = jnp.where(tile_zero + has_above > 0.0, rim_in[0, p], 0.0)
         cond_buf[own : own + R, :] = conduct_tile(slice(0, R), p)
-        cond_buf[own + R : own + R + RIM, :] = rim_in[1, p] * has_below
+        cond_buf[own + R : own + R + RIM, :] = jnp.where(tile_zero + has_below > 0.0, rim_in[1, p], 0.0)
         block = p * T + n
         right_ok, left_ok = flag(block < 2 * T - 1), flag(block > 0)
         ok = row_ok * jnp.where(lane_e < WIDTH, 1.0, jnp.where(lane_e < 96, right_ok, left_ok))
@@ -293,17 +313,31 @@
     segment, in_first = lane_8 // 16, lax.rem(lane_8, 16) < 8
     in_low = lane_8 < WIDTH
 
-    def row_copies(p, group):
-        return [
-            remote(
-                rows_out.at[p, side, group], rows_in.at[p, 1 - side, group],
-                row_send, row_recv.at[p, 1 - side], n, row,
-            )
-            for side, row in ((0, above), (1, below))
+    def halo_copies(p):
+        right, left = jnp.where(n == T - 1, 0, p), jnp.where(n == 0, 1, p)
+        sided = [
+            [
+                remote(src, dst, halo_send.at[side], recv, step, there[side][1])
+                for src, dst, recv, step in (
+                    (rows_out.at[p, side], rows_in.at[p, 1 - side], row_recv.at[p, side], n),
+                    (right_out.at[right, side], right_in.at[p, 2 + side],
+                     corner_recv.at[p, side, 0], nxt),
+                    (left_out.at[left, side], left_in.at[p, 2 + side],
+                     corner_recv.at[p, side, 1], prv),
+                )
+            ]
+            for side in range(2)
         ]
-
-    def send_rows(p):
-        def pass_rows(group, carry):
+        level = [
+            remote(right_out.at[right], right_in.at[p, pl.ds(0, 2)],
+                   col_send, col_recv.at[p, 0], nxt, sp),
+            remote(left_out.at[left], left_in.at[p, pl.ds(0, 2)],
+                   col_send, col_recv.at[p, 1], prv, sp),
+        ]
+        return sided, level
+
+    def make_halo(p):
+        def one_group(group, carry):
             for j in range(8):
                 forward_copy(gathered.at[p, 0], p, group * 8 + j, nxt).wait_recv()
             for j in range(4):
@@ -313,11 +347,34 @@
                 bottom = gathered[p, step, H - 8 : H]
                 bottom_next = gathered[p, step + 1, H - 8 : H]
                 rows_out[p, 1, group, j] = jnp.where(in_low, roll(bottom, WIDTH), bottom_next)
-            for copy in row_copies(p, group):
-                copy.start()
-            return carry
-
-        lax.fori_loop(0, T // 8, pass_rows, 0)
+            for i in range(2):
+                first = jnp.zeros((8, LANES), F32)
+                second = first
+                for j in range(8):
+                    value = gathered[p, group * 8 + j, 8 * i : 8 * i + 8]
+                    first = jnp.where(segment == j, roll(value, 16 * j - 56), first)
+                    second = jnp.where(segment == j, roll(value, 16 * j + 8), second)
+                right_out[p, i, group] = jnp.where(in_first, first, roll(second, 8))
+                left_out[p, i, group] = jnp.where(in_first, roll(first, -8), second)
+            return carry
+
+        lax.fori_loop(0, T // 8, one_group, 0)
+
+    def send_halo(p):
+        sided, level = halo_copies(p)
+        for side in range(2):
+            for copy in sided[side]:
+                when_there(side, copy.start)
+        for copy in level:
+            copy.start()
+
+    def wait_halo(p):
+        sided, level = halo_copies(p)
+        for side in range(2):
+            for copy in sided[side]:
+                when_there(1 - side, copy.wait_recv)
+        for copy in level:
+            copy.wait_recv()
 
     def packed_rows(p, group, j, i):
         if i < 2:
@@ -327,31 +384,12 @@
             return jnp.where(in_low, roll(down, WIDTH), up)
         return jnp.where(in_low, down, roll(up, WIDTH))
 
-    def pack_edges(p):
-        for side in range(2):
-            whole = rows_in.at[p, side]
-            pltpu.make_async_copy(whole, whole, row_recv.at[p, side]).wait()
-
-        def pack_group(group, carry):
-            for i in range(3):
-                first = jnp.zeros((8, LANES), F32)
-                second = first
-                for j in range(8):
-                    value = packed_rows(p, group, j, i)
-                    first = jnp.where(segment == j, roll(value, 16 * j - 56), first)
-                    second = jnp.where(segment == j, roll(value, 16 * j + 8), second)
-                right_out[p, i, group] = jnp.where(in_first, first, roll(second, 8))
-                left_out[p, i, group] = jnp.where(in_first, roll(first, -8), second)
-            return carry
-
-        lax.fori_loop(0, T // 8, pack_group, 0)
-
-    def columns_copies(p):
-        right = right_out.at[jnp.where(n == T - 1, 0, p)]
-        left = left_out.at[jnp.where(n == 0, 1, p)]
+    def packed_columns(p, group, i):
+        if i < 2:
+            return right_in[p, i, group], left_in[p, i, group]
         return (
-            remote(right, right_in.at[p], col_send.at[p, 0], col_recv.at[p, 0], nxt, sp),
-            remote(left, left_in.at[p], col_send.at[p, 1], col_recv.at[p, 1], prv, sp),
+            jnp.where(in_first, right_in[p, 2, group], right_in[p, 3, group]),
+            jnp.where(in_first, left_in[p, 3, group], left_in[p, 2, group]),
         )
 
     GROUPS = ((0, 2), (1, 3), (4, -1))
@@ -359,7 +397,7 @@
     def unpack(p):
         def unpack_group(group, carry):
             for i, (low, high) in enumerate(GROUPS):
-                from_left, from_right = right_in[p, i, group], left_in[p, i, group]
+                from_left, from_right = packed_columns(p, group, i)
                 for j in range(8):
                     step = group * 8 + j
                     value = packed_rows(p, group, j, i)
@@ -450,12 +488,14 @@
     def pack_back(p):
         lane = lane_index((H, LANES))
 
-        def pack_step(step, carry):
-            low, high = x_buf[step, own : own + H, :], x_buf[step, own + H : own + R, :]
-            back_out[p, step] = jnp.where(lane < WIDTH, low, roll(high, WIDTH))
-            return carry
-
-        lax.fori_loop(0, T, pack_step, 0)
+        def pack_steps(group, carry):
+            for j in range(8):
+                step = group * 8 + j
+                low, high = x_buf[step, own : own + H, :], x_buf[step, own + H : own + R, :]
+                back_out[p, step] = jnp.where(lane < WIDTH, low, roll(high, WIDTH))
+            return carry
+
+        lax.fori_loop(0, T // 8, pack_steps, 0)
 
     def give_back(p, start, stop):
         def send(j, carry):
@@ -501,42 +541,33 @@
 
         lax.fori_loop(0, PAIRS, step, 0)
 
-    def pass_columns(p):
-        copies = columns_copies(p)
-        for copy in copies:
-            copy.start()
-            finish.append(copy.wait_send)
-        return copies
-
-    send_rows(0)
-    pl.when(n == 0)(lambda: send_rows(1))
-    forward_some(1, 0, PAIRS // 2, only=False)
-    pack_edges(0)
-    pl.when(n == 0)(lambda: pack_edges(1))
-    first_columns = pass_columns(0)
-    forward_some(1, PAIRS // 2, PAIRS, only=False)
-    for copy in first_columns:
-        copy.wait_recv()
+    EARLY = 4
+
+    pl.when(n == 0)(lambda: make_halo(1))
+    make_halo(0)
+    send_halo(0)
+    forward_all(1, only=False, prepare=False, wait=False)
+    wait_halo(0)
     unpack(0)
     solve(0)
     pack_back(0)
 
-    pl.when(n != 0)(lambda: send_rows(1))
-    give_back(0, 0, T // 4)
-    pl.when(n != 0)(lambda: pack_edges(1))
-    second_columns = pass_columns(1)
-    give_back(0, T // 4, T // 2)
-    for copy in second_columns:
-        copy.wait_recv()
+    give_back(0, 0, EARLY)
+    pl.when(n != 0)(lambda: make_halo(1))
+    send_halo(1)
+    give_back(0, EARLY, T)
+    wait_halo(1)
     unpack(1)
-    give_back(0, T // 2, T)
     solve(1)
     pack_back(1)
     give_back(1, 0, T)
     update(0)
     update(1)
-    whole = rows_in
-    finish.append(pltpu.make_async_copy(whole, whole, row_send).wait)
+    finish.append(pltpu.make_async_copy(right_in, right_in, col_send).wait)
+    for side in range(2):
+        for sent in (rows_out.at[0], right_out):
+            wait = pltpu.make_async_copy(sent, sent, halo_send.at[side]).wait
+            finish.append(functools.partial(when_there, side, wait))
     sent = back_out.at[:, pl.ds(0, T - 1)]
     finish.append(pltpu.make_async_copy(sent, sent, back_send).wait)
     finish.append(pltpu.make_async_copy(out, out, store_sem).wait)
@@ -552,7 +583,7 @@
     dma = pltpu.SemaphoreType.DMA
     vmem = lambda *shape: pltpu.VMEM(shape, F32)
     block = (R // 2, LANES)
-    group = (T // 8, 8, LANES)
+    tile = (8, LANES)
     in_hbm = pl.BlockSpec(memory_space=pltpu.HBM)
     updated = pl.pallas_call(
         functools.partial(kernel, T, S, Z, R),
@@ -560,18 +591,19 @@
         in_specs=[in_hbm] * 3,
         out_specs=in_hbm,
         scratch_shapes=[
-            vmem(R, NC), vmem(R, NC), vmem(R, NC), vmem(R, NC),
+            vmem(R, NC), vmem(R, NC), vmem(R, NC), vmem(R, NC), vmem(R, NC),
             vmem(2, 2, NC), vmem(2, 2, NC), vmem(2, 2, RIM, LANES), vmem(2, 2, RIM, LANES),
             vmem(2, T // 2, *block), vmem(2, T // 2, *block),
             vmem(2, T // 2, *block), vmem(2, T // 2, *block),
             vmem(2, T, *block), vmem(2, 2, T // 8, 4, RIM, LANES), vmem(2, 2, T // 8, 4, RIM, LANES),
-            vmem(2, 3, *group), vmem(2, 3, *group), vmem(2, 3, *group), vmem(2, 3, *group),
+            vmem(2, 2, T // 8, *tile), vmem(2, 2, T // 8, *tile),
+            vmem(2, 4, T // 8, *tile), vmem(2, 4, T // 8, *tile),
             vmem(T, E + 16, LANES), vmem(T, E + 16, LANES), vmem(T, E, LANES),
             vmem(E + 16, LANES), vmem(2, 7, E, LANES),
             vmem(2, T, *block), vmem(2, T, *block),
             dma((3, 3)), dma, dma((2,)), dma((2,)), dma((2,)), dma((2,)),
-            dma, dma, dma((2, T // 2)), dma((2, T // 2)),
-            dma, dma((2, T)), dma, dma((2, 2)), dma((2, 2)), dma((2, 2)),
+            dma, dma, dma((2, 4)), dma((2, 4)),
+            dma, dma((2, T)), dma((2,)), dma((2, 2)), dma, dma((2, 2)), dma((2, 2, 2)),
             dma, dma((2, T)),
         ],
         compiler_params=pltpu.CompilerParams(

time: 89.4 us -> 83.1 us (0.930); the launches traced: 89.2 us -> 81.9 us
  Pallas kernels: 87.3 us -> 80 us
    pallas_call x1, Pallas kernels: 87.3 us -> 80 us  [per_device(): pl.pallas_call(functools.partial(kernel, T, S, Z, R), out_shape=jax.Shape...]
where the time goes in v3:
time: 83.1 us; the launch traced here: 81.9 us
  Pallas kernels  80 us (96%)
  local copies, waits for them, and re-layouts  1.87 us (2%)
    pallas_call x1, Pallas kernels, per_device(): pl.pallas_call(functools.partial(kernel, T, S, Z, R), out_shape=jax.Shape...  80 us
    unnamed x1, local copies, waits for them, and re-layouts  1.87 us

profile of v3, /device:TPU:6, one launch (start us, length us, event | category | flops | bytes accessed | tf_op | source)
XLA Modules:
  0.0 81.9 jit_solution(14983789185382654371)
XLA Ops:
  0.0 80.0 %shard_map.37 = f32[32,4096]{1,0:T(8,128)} custom-call(f32[32,4096]{1,0:T(8,128)} %bitcast.4, f32[32,4096]{1,0:T(8,128)} %bitcast.5, f32[32,4096]{1,0:T(8,128)} %c_hbm.1), custom_call_target="tpu_custom_call" | custom-call | tf_op jit(solution)/shard_map/pallas_call | solution.py:588
  80.1 1.9 %copy.5 = f32[1,32,4096]{2,1,0:T(8,128)} copy(f32[1,32,4096]{2,1,0:T(8,128)} %bitcast.3) | data formatting | bytes 1048576

commit v4 on v3

--- a/solution.py
+++ b/solution.py
@@ -394,57 +394,53 @@
 
     GROUPS = ((0, 2), (1, 3), (4, -1))
 
-    def unpack(p):
-        def unpack_group(group, carry):
-            for i, (low, high) in enumerate(GROUPS):
+    def over_time(body, carry):
+        for step in range(T):
+            carry = body(step, carry)
+        return carry
+
+    def wrap(p, first, rows, dst, last):
+        here = pl.ds(base + first, rows)
+        gain = coeff[p, 4, first : first + rows, :]
+
+        def body(t, carry):
+            carry = gain * carry
+            dst[t, here, :] = dst[t, here, :] + carry
+            return carry
+
+        over_time(body, last * coeff[p, 5, first : first + rows, :])
+
+    def first_sweep(p):
+        places = [place for pair in GROUPS for place in pair]
+        firsts = [RIM + 8 * place for place in places]
+        gains = [coeff[p, 4, first : first + 8, :] for first in firsts]
+        weights = [coeff[p, 6, first : first + 8, :] for first in firsts]
+
+        def one_group(group, carry):
+            carry = list(carry)
+            for i in range(3):
                 from_left, from_right = packed_columns(p, group, i)
                 for j in range(8):
                     step = group * 8 + j
                     value = packed_rows(p, group, j, i)
-                    for place, own_part, left_at, right_at in (
-                        (low, value, 0, 8),
-                        (high, roll(value, WIDTH), 8, 0),
+                    for at, own_part, left_at, right_at in (
+                        (2 * i, value, 0, 8),
+                        (2 * i + 1, roll(value, WIDTH), 8, 0),
                     ):
                         left = roll(from_left, 120 - 16 * j - left_at)
                         right = roll(from_right, 64 - 16 * j - right_at)
-                        x_buf[step, own + 8 * place : own + 8 * place + 8, :] = jnp.where(
-                            in_low, own_part, jnp.where(lane_8 < 96, right, left)
-                        )
-            return carry
-
-        lax.fori_loop(0, T // 8, unpack_group, 0)
-
-    def over_time(body, carry):
-        for step in range(T):
-            carry = body(step, carry)
-        return carry
-
-    def wrap(p, first, rows, dst, last):
-        here = pl.ds(base + first, rows)
-        gain = coeff[p, 4, first : first + rows, :]
-
-        def body(t, carry):
-            carry = gain * carry
-            dst[t, here, :] = dst[t, here, :] + carry
-            return carry
-
-        over_time(body, last * coeff[p, 5, first : first + rows, :])
-
-    def first_sweep(p, first, rows, src, dst):
-        here, q_here = pl.ds(base + first, rows), pl.ds(first, rows)
-        gain = coeff[p, 4, first : first + rows, :]
-        weight = coeff[p, 6, first : first + rows, :]
-        ok = weight > 0.0
-
-        def body(t, carry):
-            scaled = jnp.where(ok, weight * src[t, here, :], 0.0)
-            q_buf[t, q_here, :] = scaled
-            value = scaled + gain * carry
-            dst[t, here, :] = value
-            return value
-
-        last = over_time(body, jnp.zeros((rows, LANES), F32))
-        wrap(p, first, rows, dst, last)
+                        whole = jnp.where(in_low, own_part, jnp.where(lane_8 < 96, right, left))
+                        scaled = jnp.where(weights[at] > 0.0, weights[at] * whole, 0.0)
+                        first = firsts[at]
+                        q_buf[step, first : first + 8, :] = scaled
+                        carry[at] = scaled + gains[at] * carry[at]
+                        w_buf[step, base + first : base + first + 8, :] = carry[at]
+            return tuple(carry)
+
+        zero = jnp.zeros((8, LANES), F32)
+        last = lax.fori_loop(0, T // 8, one_group, (zero,) * len(places))
+        in_order = sorted(zip(firsts, last), key=lambda pair: pair[0])
+        wrap(p, 0, E, w_buf, jnp.concatenate([value for _, value in in_order], axis=0))
 
     def sweep(p, first, rows, src, dst):
         here, q_here = pl.ds(base + first, rows), pl.ds(first, rows)
@@ -468,8 +464,7 @@
     BLOCK = 24
 
     def solve(p):
-        for first, rows in blocks_of(0, E, BLOCK):
-            first_sweep(p, first, rows, x_buf, w_buf)
+        first_sweep(p)
 
         def two_sweeps(i, carry):
             for first, rows in blocks_of(0, E, BLOCK):
@@ -548,7 +543,6 @@
     send_halo(0)
     forward_all(1, only=False, prepare=False, wait=False)
     wait_halo(0)
-    unpack(0)
     solve(0)
     pack_back(0)
 
@@ -557,7 +551,6 @@
     send_halo(1)
     give_back(0, EARLY, T)
     wait_halo(1)
-    unpack(1)
     solve(1)
     pack_back(1)
     give_back(1, 0, T)

time: 83.1 us -> 83.2 us (level)
  no operation moved by 1% of the time
where the time goes in v4:
time: 83.2 us; the launch traced here: 81.7 us
  Pallas kernels  79.8 us (96%)
  local copies, waits for them, and re-layouts  1.87 us (2%)
    pallas_call x1, Pallas kernels, per_device(): pl.pallas_call(functools.partial(kernel, T, S, Z, R), out_shape=jax.Shape...  79.8 us
    unnamed x1, local copies, waits for them, and re-layouts  1.87 us

profile of v4, /device:TPU:6, one launch (start us, length us, event | category | flops | bytes accessed | tf_op | source)
XLA Modules:
  0.0 81.7 jit_solution(17096574951156868859)
XLA Ops:
  0.0 79.8 %shard_map.37 = f32[32,4096]{1,0:T(8,128)} custom-call(f32[32,4096]{1,0:T(8,128)} %bitcast.4, f32[32,4096]{1,0:T(8,128)} %bitcast.5, f32[32,4096]{1,0:T(8,128)} %c_hbm.1), custom_call_target="tpu_custom_call" | custom-call | tf_op jit(solution)/shard_map/pallas_call | solution.py:581
  79.8 1.9 %copy.5 = f32[1,32,4096]{2,1,0:T(8,128)} copy(f32[1,32,4096]{2,1,0:T(8,128)} %bitcast.3) | data formatting | bytes 1048576
